TPU v7x, 32 devices: a whole 2x2x4 slice. The times are simulated.
32 devices in a mesh: tile: 4 (over x, core), kern: 8 (over z, y).
Axes of the slice: x: 2, y: 2, z: 4, core: 2. Of those that a mesh axis runs over, the one named last changes fastest.
Arguments:
- mask: float32 [256, 2048], P('tile'), may hold values from 0 to 1
- target: int32 [256, 2048], P('tile'), may hold values 0 or 1
- kernels: bfloat16 [8, 2, 21, 21], P('kern'), may hold values from -0.25 to 0.25
- source_weight: float32 [8], replicated, may hold values from 0.2 to 2
- assign: int32 [8], P('kern'), may hold values from 0 to 7, each once
Outputs:
- mask_grad: float32 [256, 2048], P('tile', 'kern')
- resist: float32 [256, 2048], P('tile', 'kern')
Inputs may be any that keep to these rules, and one draw needn't show every extreme that they name: assign is a permutation of 0 to 7.
All inputs are finite; a program needn't handle non-finite values. No bound on the sum of `target` on one device may be relied on, other than what follows from the above.
Results may differ from a plain program's by a relative error of at most 0.0036.
Values may be sent and summed in bfloat16 or wider, within the bound.
A program may use at most 64 MiB of HBM per device.

v0:
```python
import jax
import jax.numpy as jnp
from jax import lax
from jax.sharding import PartitionSpec as P

SLOPE_FACTOR = 4.0
LEVEL_VALUE = 0.6


def padded_2(cells, sides, width):
    for axis, dim in sides:
        count = lax.axis_size(axis)
        ends = count - 1
        head = lax.slice_in_dim(cells, 0, width, axis=dim)
        tail = lax.slice_in_dim(cells, cells.shape[dim] - width, cells.shape[dim], axis=dim)
        cells = jnp.concatenate(
            [
                lax.ppermute(tail, axis, [(i, (i + 1) % count) for i in range(ends)]),
                cells,
                lax.ppermute(head, axis, [((i + 1) % count, i) for i in range(ends)]),
            ],
            axis=dim,
        )
    return cells


def windows_of(extended, col_count):
    blocks = col_count // 128
    head_shape = extended.shape[:-1]
    leading = extended[..., :col_count].reshape(head_shape + (blocks, 128))
    trailing = extended[..., 128 : col_count + 128].reshape(head_shape + (blocks, 128))
    return jnp.concatenate([leading, trailing], axis=-1)


def column_windows(padded, margin, col_count):
    widths = [(0, 0)] * (padded.ndim - 1) + [(margin, 256 - margin)]
    return windows_of(jnp.pad(padded, widths), col_count)


def select_table(span_len):
    column = jnp.arange(256)[:, None, None]
    output = jnp.arange(128)[None, :, None]
    tapped = jnp.arange(span_len)[None, None, :]
    return (column - output == tapped).astype(jnp.float32)


def forward_matrix(kernel_pair):
    span_len = kernel_pair.shape[-1]
    matrix = jnp.einsum("tij,coj->icto", kernel_pair.astype(jnp.float32), select_table(span_len))
    return matrix.reshape(span_len, 256, 256).astype(jnp.bfloat16)


def adjoint_matrix(kernel_pair):
    span_len = kernel_pair.shape[-1]
    flipped = kernel_pair[:, ::-1, ::-1]
    matrix = jnp.einsum("tij,coj->itco", flipped.astype(jnp.float32), select_table(span_len))
    return matrix.astype(jnp.bfloat16)


def forward_fields(windows, matrix, out_rows):
    blocks = windows.shape[-2]
    col_count = blocks * 128

    def forward_accumulate(offset, running):
        sliced = lax.dynamic_slice_in_dim(windows, offset, out_rows, 0)
        return running + jnp.einsum(
            "rbc,cn->rbn", sliced, matrix[offset], preferred_element_type=jnp.float32
        )

    running = lax.fori_loop(
        0, matrix.shape[0], forward_accumulate, jnp.zeros((out_rows, blocks, 256), jnp.float32)
    )
    return (
        running[..., :128].reshape(out_rows, col_count),
        running[..., 128:].reshape(out_rows, col_count),
    )


def adjoint_field(windows, matrix, out_rows):
    blocks = windows.shape[-2]
    col_count = blocks * 128

    def adjoint_accumulate(offset, running):
        sliced = lax.dynamic_slice_in_dim(windows, offset, out_rows, 0)
        return running + jnp.einsum(
            "rtbc,tcn->rbn", sliced, matrix[offset], preferred_element_type=jnp.float32
        )

    running = lax.fori_loop(
        0, matrix.shape[0], adjoint_accumulate, jnp.zeros((out_rows, blocks, 128), jnp.float32)
    )
    return running.reshape(out_rows, col_count)


def on_device(mask, target, kernels, source_weight, assign):
    own_rows = mask.shape[0]
    col_count = mask.shape[1]
    span_len = kernels.shape[-1]
    margin = (span_len - 1) // 2
    kern_count = lax.axis_size("kern")
    share = col_count // kern_count
    kern_index = lax.axis_index("kern")
    tile_index = lax.axis_index("tile")
    clip_rows = own_rows * lax.axis_size("tile")
    mask_copy = mask.astype(jnp.bfloat16)
    total = jnp.sum(source_weight)
    slot_ids = jnp.arange(source_weight.shape[0])[None, :]
    picked = (assign[:, None] == slot_ids).astype(jnp.float32)
    local_weight = jnp.sum(picked * source_weight[None, :], axis=1)
    stacked = jnp.stack([mask_copy, target.astype(jnp.bfloat16)], axis=1)
    padded = padded_2(stacked, (("tile", 0),), 2 * margin)
    out_rows = own_rows + 2 * margin
    mask_padded = padded[:, 0]
    target_rows = padded[margin : margin + out_rows, 1].astype(jnp.float32)
    global_row = tile_index * own_rows - margin + jnp.arange(out_rows)
    inside = jnp.logical_and(global_row >= 0, global_row < clip_rows)
    mask_windows = column_windows(mask_padded, margin, col_count)
    source = 0
    real_part, imag_part = forward_fields(mask_windows, forward_matrix(kernels[source]), out_rows)
    field_list = [(real_part, imag_part)]
    partial_value = local_weight[source] * (real_part * real_part + imag_part * imag_part)
    aerial = lax.psum(partial_value, "kern") / total
    resist_all = jax.nn.sigmoid(SLOPE_FACTOR * (aerial - LEVEL_VALUE))
    sense = 2.0 * (resist_all - target_rows) * SLOPE_FACTOR * resist_all * (1.0 - resist_all)
    resist_own = lax.dynamic_slice_in_dim(resist_all, kern_index * share, share, 1)
    sense = jnp.where(inside[:, None], sense, 0.0)
    resist_out = resist_own[margin : margin + own_rows]
    adjoint_list = []
    source = 0
    factor = 2.0 * local_weight[source] / total
    adjoint_list.append(factor * sense * field_list[source][0])
    adjoint_list.append(factor * sense * field_list[source][1])
    adjoints = jnp.stack(adjoint_list, axis=1).astype(jnp.bfloat16)
    source = 0
    grad_terms = adjoint_field(
        column_windows(adjoints, margin, col_count), adjoint_matrix(kernels[source]), own_rows
    )
    mask_grad = lax.psum_scatter(grad_terms, "kern", scatter_dimension=1, tiled=True)
    return (mask_grad, resist_out)


def solution(mesh):
    placed = (P("tile", None), P("tile", None), P("kern", None, None, None), P(), P("kern"))
    return jax.shard_map(
        on_device,
        mesh=mesh,
        in_specs=placed,
        out_specs=(P("tile", "kern"), P("tile", "kern")),
        check_vma=False,
    )
```

profile of v0, /device:TPU:1, one launch (start us, length us, event | category | flops | bytes accessed | tf_op | source)
XLA Modules:
  0.0 239.4 jit_solution(3003246693781639555)
XLA Ops:
  7.2 1.1 convert_bitcast_fusion.2
  8.3 1.1 convert_bitcast_fusion.3
  9.4 4.5 %collective-permute-start = (bf16[20,2,2048]{2,0,1:T(8,128)(2,1)S(1)}, bf16[20,2,2048]{2,0,1:T(8,128)(2,1)S(1)}, u32[]{:S(2)}, u32[]{:S(2)}) collective-permute-start(bf16[20,2,2048]{2,0,1:T(8,128)(2,1)S(1)} %get-tuple-element.228), channel_id=1, source_target_pairs={{0,8},{8,16},{16,24},{1,9},{9,17},{17,25},{2,10},{10,18},{18,26},{... | collective-permute-start | bytes 491528 | tf_op jit(solution)/shard_map/ppermute | solution.py:18
  13.9 1.9 collective-permute-start.1
  15.9 2.6 %convert_bitcast_fusion.1 = bf16[21,256,2,128]{3,0,2,1:T(8,128)(2,1)} fusion(s32[256,128]{1,0:T(8,128)S(1)} %iota_subtract_fusion, bf16[2,21,21]{2,0,1:T(2,128)(2,1)S(1)} %bitcast.98), kind=kOutput, calls=%fused_computation.12 | convolution fusion | flops 59867136 | bytes 2885348 | tf_op jit(solution)/shard_map/tij,coj->icto/dot_general | solution.py:49
  18.5 5.0 %copy.13 = bf16[21,256,2,128]{1,3,2,0:T(8,128)(2,1)} copy(bf16[21,256,2,128]{3,0,2,1:T(8,128)(2,1)} %convert_bitcast_fusion.1) | data formatting | bytes 5505024 | tf_op jit(solution)/shard_map/convert_element_type | solution.py:50
  24.2 0.7 fusion.38
  25.8 31.4 %while.28 = (s32[]{:T(128)}, f32[84,16,256]{2,1,0:T(8,128)S(1)}, bf16[104,16,256]{2,1,0:T(8,128)(2,1)S(1)}, bf16[21,256,256]{1,2,0:T(8,128)(2,1)}, s32[]{:T(128)}, /*index=5*/s32[]{:T(128)}) while((s32[]{:T(128)}, f32[84,16,256]{2,1,0:T(8,128)S(1)}, bf16[104,16,256]{2,1,0:T(8,128)(2,1)S(1)}, bf16[21,256,256]{1,2,0:T(8,128)(2,1)}, ...), condition=%wide.region_3.4_spmd.clone, body=%wide.region_2.3_spmd.clone.sunk | while | flops 176848896 | bytes 3572815 | solution.py:70
  25.8 1.5 convolution_add_fusion.2
  27.3 1.5 convolution_add_fusion.2
  28.8 1.5 convolution_add_fusion.2
  30.3 1.5 convolution_add_fusion.2
  31.8 1.5 convolution_add_fusion.2
  33.3 1.5 convolution_add_fusion.2
  34.8 1.5 convolution_add_fusion.2
  36.3 1.5 convolution_add_fusion.2
  37.8 1.5 convolution_add_fusion.2
  39.3 1.5 convolution_add_fusion.2
  40.8 1.5 convolution_add_fusion.2
  42.3 1.5 convolution_add_fusion.2
  43.8 1.5 convolution_add_fusion.2
  45.3 1.5 convolution_add_fusion.2
  46.8 1.5 convolution_add_fusion.2
  48.2 1.5 convolution_add_fusion.2
  49.7 1.5 convolution_add_fusion.2
  51.2 1.5 convolution_add_fusion.2
  52.7 1.5 convolution_add_fusion.2
  54.2 1.5 convolution_add_fusion.2
  55.7 1.5 convolution_add_fusion.2
  57.9 1.6 add_multiply_fusion
  60.4 1.0 convert_bitcast_fusion
  61.4 2.3 copy.17
  64.4 69.4 %all-reduce.4.cloned.1.call-done = f32[84,2048]{1,0:T(8,128)} async-done(((f32[84,2048]{1,0:T(8,128)}), f32[84,2048]{1,0:T(8,128)}) %all-reduce.4.cloned.1.call-update) | async-done | bytes 688144 | tf_op jit(solution)/shard_map/psum | solution.py:122
  133.8 2.3 fusion.31
  136.0 0.3 fusion.32
  136.4 0.4 fusion.23
  136.9 1.2 reshape.63
  138.1 1.2 reshape.64
  139.3 1.5 pad_maximum_fusion
  140.8 29.8 %while.29 = (s32[]{:T(128)}, f32[64,16,128]{2,1,0:T(8,128)S(1)}, bf16[84,2,16,256]{3,2,0,1:T(8,128)(2,1)S(1)}, bf16[21,2,256,128]{3,2,1,0:T(8,128)(2,1)}, s32[]{:T(128)}, /*index=5*/s32[]{:T(128)}) while((s32[]{:T(128)}, f32[64,16,128]{2,1,0:T(8,128)S(1)}, bf16[84,2,16,256]{3,2,0,1:T(8,128)(2,1)S(1)}, ...), condition=%wide.region_6.7_spmd.clone, body=%wide.region_5.6_spmd.clone.sunk | while | flops 134479872 | bytes 2229327 | solution.py:89
  140.8 1.4 fusion.50
  142.2 1.4 fusion.50
  143.6 1.4 fusion.50
  145.1 1.4 fusion.50
  146.5 1.4 fusion.50
  147.9 1.4 fusion.50
  149.3 1.4 fusion.50
  150.8 1.4 fusion.50
  152.2 1.4 fusion.50
  153.6 1.4 fusion.50
  155.0 1.4 fusion.50
  156.4 1.4 fusion.50
  157.9 1.4 fusion.50
  159.3 1.4 fusion.50
  160.7 1.4 fusion.50
  162.1 1.4 fusion.50
  163.5 1.4 fusion.50
  164.9 1.4 fusion.50
  166.4 1.4 fusion.50
  167.8 1.4 fusion.50
  169.2 1.4 fusion.50
  170.6 1.0 copy.36
  171.6 0.7 dynamic-slice
  172.3 60.2 %reduce-scatter.2.cloned.1.call-done = f32[64,256]{1,0:T(8,128)} async-done(((f32[64,2048]{1,0:T(8,128)}), f32[64,256]{1,0:T(8,128)}) %reduce-scatter.2.cloned.1.call-update) | async-done | bytes 65552 | tf_op jit(solution)/shard_map/reduce_scatter | solution.py:138
  (32 shorter events, 2.1 us)
Async XLA Ops:
  7.2 8.7 %copy-start.2 = (bf16[1,2,21,21]{3,1,2,0:T(2,128)(2,1)S(1)}, bf16[1,2,21,21]{3,1,2,0:T(2,128)(2,1)}, u32[]{:S(2)}) copy-start(bf16[1,2,21,21]{3,1,2,0:T(2,128)(2,1)} %param.11) | copy-start | bytes 5296
  7.2 126.6 %all-reduce.4.cloned.1.call-start = ((), (), s32[]{:S(2)}) async-start(), calls=%async_computation.1 | async-start | bytes 1441792 | tf_op jit(solution)/shard_map/psum | solution.py:122
  9.4 15.4 %collective-permute-start = (bf16[20,2,2048]{2,0,1:T(8,128)(2,1)S(1)}, bf16[20,2,2048]{2,0,1:T(8,128)(2,1)S(1)}, u32[]{:S(2)}, u32[]{:S(2)}) collective-permute-start(bf16[20,2,2048]{2,0,1:T(8,128)(2,1)S(1)} %get-tuple-element.228), channel_id=1, source_target_pairs={{0,8},{8,16},{16,24},{1,9},{9,17},{17,25},{2,10},{10,18},{18,26},{... | collective-permute-start | bytes 491528 | tf_op jit(solution)/shard_map/ppermute | solution.py:18
  13.9 10.9 %collective-permute-start.1 = (bf16[20,2,2048]{2,0,1:T(8,128)(2,1)S(1)}, bf16[20,2,2048]{2,0,1:T(8,128)(2,1)S(1)}, u32[]{:S(2)}, u32[]{:S(2)}) collective-permute-start(bf16[20,2,2048]{2,0,1:T(8,128)(2,1)S(1)} %get-tuple-element.229), channel_id=1, source_target_pairs={{8,0},{16,8},{24,16},{9,1},{17,9},{25,17},{10,2},{18,10},{26,18},{... | collective-permute-start | bytes 491528 | tf_op jit(solution)/shard_map/ppermute | solution.py:20
  18.5 5.6 %copy-start.3 = (f32[8]{0:T(128)S(1)}, f32[8]{0:T(128)}, u32[]{:S(2)}) copy-start(f32[8]{0:T(128)} %param.12) | copy-start | bytes 100
  24.8 0.7 copy-start
  59.6 173.0 %reduce-scatter.2.cloned.1.call-start = ((), (), s32[]{:S(2)}) async-start(), calls=%async_computation.2 | async-start | bytes 589824 | tf_op jit(solution)/shard_map/reduce_scatter | solution.py:138
  133.8 2.3 copy-start.1
Sparse Core Ops, SparseCore 0:
  59.7 74.0 all-reduce.3
  171.7 60.7 reduce-scatter.1
where the time goes:
time: 243 us; the launch traced here: 239 us
  waiting for transfers between devices  130 us (53%)
  matrix products  63.8 us (26%)
  between operations  16.3 us (7%)
  local copies, waits for them, and re-layouts  12.9 us (5%)
  other arithmetic  9.24 us (4%)
  starting transfers between devices  6.51 us (3%)
    psum x1, waiting for transfers between devices, on_device(): aerial = lax.psum(partial_value, 'kern') / total  69.4 us
    reduce_scatter x1, waiting for transfers between devices, on_device(): lax.psum_scatter(grad_terms, 'kern', scatter_dimension=1, tiled=True)  60.2 us
    dot_general x21, matrix products, forward_accumulate(): jnp.einsum('rbc,cn->rbn', sliced, matrix[offset], preferred_element_type=...  30.9 us
    dot_general x21, matrix products, adjoint_accumulate(): jnp.einsum('rtbc,tcn->rbn', sliced, matrix[offset], preferred_element_typ...  29.3 us
    convert_element_type x1, local copies, waits for them, and re-layouts, forward_matrix(): return matrix.reshape(span_len, 256, 256).astype(jnp.bfloat16)  4.99 us
  transfers between devices with their start and end apart: 4, of which 2 were waited for; matrix products, arithmetic and copies ran while one was open for 5% of the time, Pallas kernels for 0%

commit v1 on v0

v1 whole, which is shorter than its diff:
```python
import functools

import jax
import jax.numpy as jnp
from jax import lax
from jax.experimental import pallas as pl
from jax.experimental.pallas import tpu as pltpu
from jax.sharding import PartitionSpec as P

SLOPE_FACTOR = 4.0
LEVEL_VALUE = 0.6
PITCH = 64
HALO = 32
MESH = pl.DeviceIdType.MESH


def exchange_kernel(
    kern_count, tile_count, image_ref, taps_ref, all_taps, above, below,
    tap_send, tap_recv, halo_send, halo_recv, own_sem,
):
    tile = lax.axis_index("tile")
    kern = lax.axis_index("kern")
    rows = image_ref.shape[1]
    up = lax.rem(tile + tile_count - 1, tile_count)
    down = lax.rem(tile + 1, tile_count)
    barrier = pltpu.get_barrier_semaphore()
    for step in range(1, kern_count):
        peer = lax.rem(kern + step, kern_count)
        pl.semaphore_signal(barrier, inc=1, device_id=(tile, peer), device_id_type=MESH)
    for neighbour in (up, down):
        pl.semaphore_signal(barrier, inc=1, device_id=(neighbour, kern), device_id_type=MESH)
    own = pltpu.make_async_copy(taps_ref, all_taps.at[kern], own_sem)
    own.start()
    pl.semaphore_wait(barrier, kern_count - 1 + 2)
    copies = []
    for step in range(1, kern_count):
        peer = lax.rem(kern + step, kern_count)
        copies.append(
            pltpu.make_async_remote_copy(
                src_ref=taps_ref,
                dst_ref=all_taps.at[kern],
                send_sem=tap_send.at[step],
                recv_sem=tap_recv.at[step],
                device_id=(tile, peer),
                device_id_type=MESH,
            )
        )
    copies.append(
        pltpu.make_async_remote_copy(
            src_ref=image_ref.at[:, pl.ds(rows - HALO, HALO), :],
            dst_ref=above,
            send_sem=halo_send.at[0],
            recv_sem=halo_recv.at[0],
            device_id=(down, kern),
            device_id_type=MESH,
        )
    )
    copies.append(
        pltpu.make_async_remote_copy(
            src_ref=image_ref.at[:, pl.ds(0, HALO), :],
            dst_ref=below,
            send_sem=halo_send.at[1],
            recv_sem=halo_recv.at[1],
            device_id=(up, kern),
            device_id_type=MESH,
        )
    )
    for copy in copies:
        copy.start()
    own.wait()
    for copy in copies:
        copy.wait()


def compute_kernel(
    span, share, clip_rows, clip_cols, image_ref, taps_ref, above_ref, below_ref,
    grad_out, resist_out, mask_rows, target_rows, toeplitz, shifted, fields, adjoint, spread,
    resist_rows, grad_rows,
):
    tile = lax.axis_index("tile")
    kern = lax.axis_index("kern")
    rows, width = image_ref.shape[1:]
    margin = (span - 1) // 2
    half = (rows + 2 * margin) // 2
    padded = -(-half // 8) * 8
    source_count = taps_ref.shape[0]
    part_count = 2 * source_count
    depth = taps_ref.shape[2]

    for held, plane in ((mask_rows, 0), (target_rows, 1)):
        keep_above = (tile > 0).astype(jnp.float32)
        keep_below = (tile < lax.axis_size("tile") - 1).astype(jnp.float32)
        held[0:HALO, :] = above_ref[plane].astype(jnp.float32) * keep_above
        held[HALO : HALO + rows, :] = image_ref[plane].astype(jnp.float32)
        held[HALO + rows :, :] = below_ref[plane].astype(jnp.float32) * keep_below

    for source in range(source_count):
        for part in range(2):
            first = (2 * source + part) * padded
            for chunk in range(depth // 128):
                lanes = slice(chunk * 128, (chunk + 1) * 128)
                row = jnp.broadcast_to(taps_ref[source, part : part + 1, lanes], (padded, 128))
                turned = pltpu.roll(row, 0, 1, stride=1, stride_axis=0)
                toeplitz[first : first + padded, lanes] = turned.astype(jnp.bfloat16)

    for block in range(2):
        top = HALO - 2 * margin + block * half
        window = mask_rows[top : top + PITCH, :]
        lanes = slice(block * width, (block + 1) * width)
        for column in range(span):
            turned = window if column == 0 else pltpu.roll(window, width - column, 1)
            shifted[column * PITCH : (column + 1) * PITCH, lanes] = turned.astype(jnp.bfloat16)
        shifted[span * PITCH :, lanes] = jnp.zeros((depth - span * PITCH, width), jnp.bfloat16)

    fields[...] = jnp.dot(toeplitz[...], shifted[...], preferred_element_type=jnp.float32)

    row_at = lax.broadcasted_iota(jnp.int32, (padded, width), 0)
    col_at = lax.broadcasted_iota(jnp.int32, (padded, width), 1)
    clip_col = kern * share - margin + col_at
    col_inside = jnp.logical_and(clip_col >= 0, clip_col < clip_cols)
    for block in range(2):
        lanes = slice(block * width, (block + 1) * width)
        aerial = jnp.zeros((padded, width), jnp.float32)
        for source in range(source_count):
            weight = taps_ref[source, 2:3, 0:width]
            first = 2 * source * padded
            real = fields[first : first + padded, lanes]
            imag = fields[first + padded : first + 2 * padded, lanes]
            aerial = aerial + weight * (real * real + imag * imag)
        resist = 1.0 / (1.0 + jnp.exp(-SLOPE_FACTOR * (aerial - LEVEL_VALUE)))
        resist_rows[block * half : block * half + padded, :] = resist
        top = HALO - margin + block * half
        target = pltpu.roll(target_rows[top : top + padded, :], width - margin, 1)
        sense = 2.0 * (resist - target) * SLOPE_FACTOR * resist * (1.0 - resist)
        clip_row = tile * rows - margin + block * half + row_at
        inside = jnp.logical_and(jnp.logical_and(clip_row >= 0, clip_row < clip_rows), row_at < half)
        sense = jnp.where(jnp.logical_and(inside, col_inside), sense, 0.0)
        for source in range(source_count):
            weight = taps_ref[source, 2:3, 0:width]
            scaled = 2.0 * weight * sense
            for part in range(2):
                first = (2 * source + part) * padded
                adjoint[first : first + padded, lanes] = (
                    scaled * fields[first : first + padded, lanes]
                ).astype(jnp.bfloat16)
    resist_out[...] = pltpu.roll(resist_rows[margin : margin + rows, :], width - margin, 1)[:, :share]

    spread[...] = lax.dot_general(
        toeplitz[...], adjoint[...], (((0,), (0,)), ((), ())), preferred_element_type=jnp.float32
    )

    grads = []
    for block in range(2):
        lanes = slice(block * width, (block + 1) * width)
        total = spread[0:PITCH, lanes]
        for column in range(1, span):
            total = total + pltpu.roll(
                spread[column * PITCH : (column + 1) * PITCH, lanes], column, 1
            )
        grads.append(total)
    grad_rows[...] = jnp.zeros_like(grad_rows)
    grad_rows[0:PITCH, :] = grads[0]
    grad_rows[half : half + PITCH, :] += grads[1]
    grad_out[...] = pltpu.roll(
        grad_rows[2 * margin : 2 * margin + rows, :], width - 2 * margin, 1
    )[:, :share]


def on_device(mask, target, kernels, source_weight, assign):
    rows, col_count = mask.shape
    span = kernels.shape[-1]
    margin = (span - 1) // 2
    kern_count = lax.axis_size("kern")
    tile_count = lax.axis_size("tile")
    share = col_count // kern_count
    kern = lax.axis_index("kern")
    width = -(-(share + 4 * margin) // 128) * 128
    columns = span + span % 2
    depth = columns * PITCH
    half = (rows + 2 * margin) // 2
    padded = -(-half // 8) * 8
    parts = 2 * kern_count

    both = jnp.stack([mask.astype(jnp.bfloat16), target.astype(jnp.bfloat16)])
    both = jnp.pad(both, ((0, 0), (0, 0), (2 * margin, width)))
    image = lax.dynamic_slice_in_dim(both, kern * share, width, 2)
    picked = (assign[0] == jnp.arange(source_weight.shape[0])).astype(jnp.float32)
    weight = jnp.sum(picked * source_weight) / jnp.sum(source_weight)
    taps = jnp.swapaxes(kernels[0].astype(jnp.float32), 1, 2)
    taps = jnp.pad(taps, ((0, 0), (0, columns - span), (0, PITCH - span))).reshape(2, depth)
    taps = jnp.concatenate([taps, jnp.full((1, depth), weight, jnp.float32)])

    in_vmem = pl.BlockSpec(memory_space=pltpu.VMEM)
    all_taps, above, below = pl.pallas_call(
        functools.partial(exchange_kernel, kern_count, tile_count),
        out_shape=(
            jax.ShapeDtypeStruct((kern_count, 3, depth), jnp.float32),
            jax.ShapeDtypeStruct((2, HALO, width), jnp.bfloat16),
            jax.ShapeDtypeStruct((2, HALO, width), jnp.bfloat16),
        ),
        in_specs=[in_vmem] * 2,
        out_specs=(in_vmem,) * 3,
        scratch_shapes=[
            pltpu.SemaphoreType.DMA((kern_count,)),
            pltpu.SemaphoreType.DMA((kern_count,)),
            pltpu.SemaphoreType.DMA((2,)),
            pltpu.SemaphoreType.DMA((2,)),
            pltpu.SemaphoreType.DMA,
        ],
        compiler_params=pltpu.CompilerParams(collective_id=0, has_side_effects=True),
        name="exchange",
    )(image, taps)

    return pl.pallas_call(
        functools.partial(compute_kernel, span, share, rows * tile_count, col_count),
        out_shape=(
            jax.ShapeDtypeStruct((rows, share), jnp.float32),
            jax.ShapeDtypeStruct((rows, share), jnp.float32),
        ),
        in_specs=[in_vmem] * 4,
        out_specs=(in_vmem,) * 2,
        scratch_shapes=[
            pltpu.VMEM((rows + 2 * HALO, width), jnp.float32),
            pltpu.VMEM((rows + 2 * HALO, width), jnp.float32),
            pltpu.VMEM((parts * padded, depth), jnp.bfloat16),
            pltpu.VMEM((depth, 2 * width), jnp.bfloat16),
            pltpu.VMEM((parts * padded, 2 * width), jnp.float32),
            pltpu.VMEM((parts * padded, 2 * width), jnp.bfloat16),
            pltpu.VMEM((depth, 2 * width), jnp.float32),
            pltpu.VMEM((half + padded, width), jnp.float32),
            pltpu.VMEM((half + PITCH, width), jnp.float32),
        ],
        compiler_params=pltpu.CompilerParams(vmem_limit_bytes=56 * 1024 * 1024),
        name="image_gradient",
    )(image, all_taps, above, below)


def solution(mesh):
    placed = (P("tile", None), P("tile", None), P("kern", None, None, None), P(), P("kern"))
    return jax.shard_map(
        on_device,
        mesh=mesh,
        in_specs=placed,
        out_specs=(P("tile", "kern"), P("tile", "kern")),
        check_vma=False,
    )
```

time: 243 us -> 24.6 us (0.10)
  the two profiles are of different devices: /device:TPU:1 before, /device:TPU:0 now
where the time goes in v1:
time: 24.6 us; the launch traced here: 24.3 us
  Pallas kernels  18.1 us (74%)
  between operations  2.74 us (11%)
  other arithmetic  2.62 us (11%)
  local copies, waits for them, and re-layouts  0.88 us (4%)
    pallas_call x1, Pallas kernels, on_device(): pl.pallas_call(functools.partial(exchange_kernel, kern_count, tile_count)...  11.8 us
    pallas_call x1, Pallas kernels, on_device(): pl.pallas_call(functools.partial(compute_kernel, span, share, rows * tile...  6.27 us
    another operation x3, other arithmetic, on_device(): both = jnp.stack([mask.astype(jnp.bfloat16), target.astype(jnp.bfloat16)])  1.92 us
    reduce_sum x1, other arithmetic, on_device(): weight = jnp.sum(picked * source_weight) / jnp.sum(source_weight)  0.68 us
    concatenate x1, local copies, waits for them, and re-layouts, on_device(): taps = jnp.concatenate([taps, jnp.full((1, depth), weight, jnp.float32)])  0.62 us

profile of v1, /device:TPU:0, one launch (start us, length us, event | category | flops | bytes accessed | tf_op | source)
XLA Modules:
  0.0 24.3 jit_solution(7643445401842272054)
XLA Ops:
  0.6 0.0 copy-start
  0.6 1.1 %convert_bitcast_fusion = bf16[1,64,2048]{2,1,0:T(8,128)(2,1)S(1)} fusion(s32[64,2048]{1,0:T(8,128)} %param.6), kind=kLoop, calls=%fused_computation.2 | loop fusion | flops 131072 | bytes 786432 | tf_op jit(solution)/shard_map/stack | solution.py:184
  1.8 0.1 copy-done
  1.9 0.0 copy-start.2
  1.9 0.8 %fusion.4.image_ref = bf16[2,64,384]{2,1,0:T(8,128)(2,1)} fusion(s32[]{:T(128)S(6)} %select_n.3, bf16[1,64,2048]{2,1,0:T(8,128)(2,1)S(1)} %convert_bitcast_fusion.1, bf16[1,64,2048]{2,1,0:T(8,128)(2,1)S(1)} %convert_bitcast_fusion), kind=kLoop, calls=%fused_computation.9 | loop fusion | flops 491520 | bytes 623616 | tf_op jit(solution)/shard_map/stack | solution.py:184
  2.6 0.0 copy-start.1
  3.3 0.0 copy-done.2
  3.3 0.7 %fusion.7 = (f32[]{:T(128)}, f32[]{:T(128)}) fusion(f32[8]{0:T(128)S(1)} %copy-done.2, s32[]{:T(128)} %bitcast.8), kind=kLoop, calls=%fused_computation.14 | loop fusion | flops 30 | bytes 44 | tf_op jit(solution)/shard_map/reduce_sum | solution.py:188
  5.4 0.0 copy-done.1
  5.4 0.1 copy.9
  5.5 0.1 reshape.15
  5.6 0.6 %concatenate.3.taps_ref = f32[3,1408]{1,0:T(4,128)} pad(f32[2,1408]{1,0:T(2,128)S(1)} %reshape.15, f32[]{:T(128)S(6)} %div.3), padding=0_1x0_0 | pad | bytes 28164 | tf_op jit(solution)/shard_map/concatenate | solution.py:191
  6.2 11.8 %exchange.1 = (f32[8,3,1408]{2,1,0:T(4,128)}, bf16[2,32,384]{2,1,0:T(8,128)(2,1)}, bf16[2,32,384]{2,1,0:T(8,128)(2,1)}) custom-call(bf16[2,64,384]{2,1,0:T(8,128)(2,1)} %fusion.4.image_ref, f32[3,1408]{1,0:T(4,128)} %concatenate.3.taps_ref), custom_call_target="tpu_custom_call" | custom-call | tf_op jit(solution)/shard_map/exchange/pallas_call | solution.py:194
  18.1 6.3 %image_gradient.1 = (f32[64,256]{1,0:T(8,128)}, f32[64,256]{1,0:T(8,128)}) custom-call(bf16[2,64,384]{2,1,0:T(8,128)(2,1)} %fusion.4.image_ref, f32[8,3,1408]{2,1,0:T(4,128)} %get-tuple-element.5.taps_ref, bf16[2,32,384]{2,1,0:T(8,128)(2,1)} %get-tuple-element.6.above_ref, bf16[2,32,384]{2,1,0:T(8,128)(2,1)} %get-tuple-element.7.below_ref), custom_call_target="tpu_custom_call" | custom-call | tf_op jit(solution)/shard_map/image_gradient/pallas_call | solution.py:214
  (3 shorter events, 0.0 us)
Async XLA Ops:
  0.6 1.2 %copy-start = (f32[64,2048]{1,0:T(8,128)S(1)}, f32[64,2048]{1,0:T(8,128)}, u32[]{:S(2)}) copy-start(f32[64,2048]{1,0:T(8,128)} %param.5) | copy-start | bytes 1572868
  1.9 1.4 %copy-start.2 = (f32[8]{0:T(128)S(1)}, f32[8]{0:T(128)}, u32[]{:S(2)}) copy-start(f32[8]{0:T(128)} %param.8) | copy-start | bytes 100
  2.6 2.7 %copy-start.1 = (bf16[1,2,21,21]{3,1,2,0:T(2,128)(2,1)S(1)}, bf16[1,2,21,21]{3,1,2,0:T(2,128)(2,1)}, u32[]{:S(2)}) copy-start(bf16[1,2,21,21]{3,1,2,0:T(2,128)(2,1)} %param.7) | copy-start | bytes 5296

commit v2 on v1

v2 whole, which is shorter than its diff:
```python
import functools

import jax
import jax.numpy as jnp
from jax import lax
from jax.experimental import pallas as pl
from jax.experimental.pallas import tpu as pltpu
from jax.sharding import PartitionSpec as P

SLOPE_FACTOR = 4.0
LEVEL_VALUE = 0.6
PITCH = 64
MASK_HALO = 32
TARGET_HALO = 16
SEGMENT = 32
MESH = pl.DeviceIdType.MESH
IN_VMEM = pl.BlockSpec(memory_space=pltpu.VMEM)


def slot_of(column):
    if column < 8:
        return 2 * column
    if column < 16:
        return 2 * (column - 8) + 1
    if column < 19:
        return 16 + 2 * (column - 16)
    return 17 + 2 * (column - 19)


def gradient_kernel(
    sizes, mask_hbm, target_hbm, kernel_ref, weight_ref, assign_ref, grad_out, resist_out,
    mask_window, target_window, send_up, send_down, above, below, square, own_taps, all_taps,
    mask_rows, target_rows, toeplitz, shifted, fields, adjoint, spread, resist_rows, grad_rows,
    load_sem, tap_send, tap_recv, halo_send, halo_recv,
):
    kern_count, tile_count, span, share, width = sizes
    tile = lax.axis_index("tile")
    kern = lax.axis_index("kern")
    rows, clip_cols = mask_hbm.shape
    clip_rows = rows * tile_count
    margin = (span - 1) // 2
    half = (rows + 2 * margin) // 2
    padded = -(-half // 8) * 8
    depth = toeplitz.shape[1]
    has_up = tile > 0
    has_down = tile < tile_count - 1

    barrier = pltpu.get_barrier_semaphore()
    for step in range(1, kern_count):
        peer = lax.rem(kern + step, kern_count)
        pl.semaphore_signal(barrier, inc=1, device_id=(tile, peer), device_id_type=MESH)

    @pl.when(has_up)
    def _():
        pl.semaphore_signal(barrier, inc=1, device_id=(tile - 1, kern), device_id_type=MESH)

    @pl.when(has_down)
    def _():
        pl.semaphore_signal(barrier, inc=1, device_id=(tile + 1, kern), device_id_type=MESH)

    start = kern * share - 2 * margin
    loaded = width + 128
    base = (start + 128) // 128 * 128 - 128
    base = jnp.minimum(jnp.maximum(base, 0), clip_cols - loaded)
    base = pl.multiple_of(base, 128)
    loads = [
        pltpu.make_async_copy(mask_hbm.at[:, pl.ds(base, loaded)], mask_window, load_sem.at[0]),
        pltpu.make_async_copy(target_hbm.at[:, pl.ds(base, loaded)], target_window, load_sem.at[1]),
    ]
    for load in loads:
        load.start()

    square[...] = jnp.zeros_like(square)
    for row in range(span):
        pair = kernel_ref[row].astype(jnp.float32)
        square[0, row : row + 1, 0:span] = pair[0:1]
        square[1, row : row + 1, 0:span] = pair[1:2]
    lane = lax.broadcasted_iota(jnp.int32, (8, 128), 1)
    packed = []
    for part in range(2):
        turned = square[part].T
        block = turned[0:8]
        block = block + pltpu.roll(turned[8:16], SEGMENT, 1)
        block = block + pltpu.roll(turned[16:24], 2 * SEGMENT, 1)
        packed.append(jnp.where(lane < 3 * SEGMENT, block, assign_ref[0].astype(jnp.float32)))
    own_taps[...] = jnp.concatenate(packed).astype(jnp.bfloat16)

    for load in loads:
        load.wait()
    clip_col = start + lax.broadcasted_iota(jnp.int32, (rows, width), 1)
    col_inside = jnp.logical_and(clip_col >= 0, clip_col < clip_cols)
    back = lax.rem(base - start + loaded, loaded)
    mask_own = pltpu.roll(mask_window[...], back, 1)[:, :width]
    mask_own = jnp.where(col_inside, mask_own, 0.0).astype(jnp.bfloat16)
    target_own = pltpu.roll(target_window[...].astype(jnp.float32), back, 1)[:, :width]
    target_own = target_own.astype(jnp.bfloat16)
    send_up[0:MASK_HALO, :] = mask_own[0:MASK_HALO]
    send_up[MASK_HALO:, :] = target_own[0:TARGET_HALO]
    send_down[0:MASK_HALO, :] = mask_own[rows - MASK_HALO :]
    send_down[MASK_HALO:, :] = target_own[rows - TARGET_HALO :]

    pl.semaphore_wait(barrier, kern_count - 1 + has_up.astype(jnp.int32) + has_down.astype(jnp.int32))
    tap_copies = []
    for step in range(1, kern_count):
        peer = lax.rem(kern + step, kern_count)
        tap_copies.append(
            pltpu.make_async_remote_copy(
                src_ref=own_taps,
                dst_ref=all_taps.at[kern],
                send_sem=tap_send.at[step],
                recv_sem=tap_recv.at[step],
                device_id=(tile, peer),
                device_id_type=MESH,
            )
        )
    upward = pltpu.make_async_remote_copy(
        src_ref=send_up,
        dst_ref=below,
        send_sem=halo_send.at[0],
        recv_sem=halo_recv.at[0],
        device_id=(tile - 1, kern),
        device_id_type=MESH,
    )
    downward = pltpu.make_async_remote_copy(
        src_ref=send_down,
        dst_ref=above,
        send_sem=halo_send.at[1],
        recv_sem=halo_recv.at[1],
        device_id=(tile + 1, kern),
        device_id_type=MESH,
    )
    pl.when(has_up)(upward.start)
    pl.when(has_down)(downward.start)
    for copy in tap_copies:
        copy.start()
    all_taps[kern] = own_taps[...]

    mask_rows[MASK_HALO : MASK_HALO + rows, :] = mask_own.astype(jnp.float32)
    target_rows[TARGET_HALO : TARGET_HALO + rows, :] = target_own.astype(jnp.float32)

    @pl.when(has_up)
    def _():
        downward.wait_recv()

    @pl.when(jnp.logical_not(has_up))
    def _():
        above[...] = jnp.zeros_like(above)

    @pl.when(has_down)
    def _():
        upward.wait_recv()

    @pl.when(jnp.logical_not(has_down))
    def _():
        below[...] = jnp.zeros_like(below)

    mask_rows[0:MASK_HALO, :] = above[0:MASK_HALO, :].astype(jnp.float32)
    mask_rows[MASK_HALO + rows :, :] = below[0:MASK_HALO, :].astype(jnp.float32)
    target_rows[0:TARGET_HALO, :] = above[MASK_HALO:, :].astype(jnp.float32)
    target_rows[TARGET_HALO + rows :, :] = below[MASK_HALO:, :].astype(jnp.float32)

    for block in range(2):
        top = MASK_HALO - 2 * margin + block * half
        window = mask_rows[top : top + PITCH, :]
        lanes = slice(block * width, (block + 1) * width)
        for column in range(span):
            turned = window if column == 0 else pltpu.roll(window, width - column, 1)
            place = slot_of(column) * PITCH
            shifted[place : place + PITCH, lanes] = turned.astype(jnp.bfloat16)
        shifted[span * PITCH :, lanes] = jnp.zeros((depth - span * PITCH, width), jnp.bfloat16)

    for copy in tap_copies:
        copy.wait_recv()
    weights = weight_ref[...]
    total = jnp.sum(weights, axis=1, keepdims=True)
    slot_ids = lax.broadcasted_iota(jnp.int32, weights.shape, 1).astype(jnp.float32)
    first_part = lane < SEGMENT
    second_part = jnp.logical_and(lane >= 2 * SEGMENT, lane < 3 * SEGMENT)
    shares = []
    for source in range(kern_count):
        block = all_taps[source].astype(jnp.float32)
        picked = jnp.where(slot_ids == block[0:1, 3 * SEGMENT : 3 * SEGMENT + 1], weights, 0.0)
        shares.append(jnp.sum(picked, axis=1, keepdims=True) / total)
        for part in range(2):
            taps = block[8 * part : 8 * part + 8]
            near = jnp.where(
                first_part, taps, jnp.where(second_part, pltpu.roll(taps, SEGMENT, 1), 0.0)
            )
            far = jnp.where(first_part, pltpu.roll(taps, 2 * SEGMENT, 1), 0.0)
            last = jnp.where(second_part, taps, 0.0)
            first = (2 * source + part) * padded
            for chunk in range(depth // 128):
                if chunk < 8:
                    row = near[chunk : chunk + 1]
                else:
                    row = far[chunk - 8 : chunk - 7] + last[chunk - 5 : chunk - 4]
                row = jnp.broadcast_to(row, (padded, 128))
                turned = pltpu.roll(row, 0, 1, stride=1, stride_axis=0)
                lanes = slice(chunk * 128, (chunk + 1) * 128)
                toeplitz[first : first + padded, lanes] = turned.astype(jnp.bfloat16)

    fields[...] = jnp.dot(toeplitz[...], shifted[...], preferred_element_type=jnp.float32)

    row_at = lax.broadcasted_iota(jnp.int32, (padded, width), 0)
    col_at = lax.broadcasted_iota(jnp.int32, (padded, width), 1)
    clip_col = kern * share - margin + col_at
    col_inside = jnp.logical_and(clip_col >= 0, clip_col < clip_cols)
    for block in range(2):
        lanes = slice(block * width, (block + 1) * width)
        aerial = jnp.zeros((padded, width), jnp.float32)
        for source in range(kern_count):
            first = 2 * source * padded
            real = fields[first : first + padded, lanes]
            imag = fields[first + padded : first + 2 * padded, lanes]
            aerial = aerial + shares[source] * (real * real + imag * imag)
        resist = 1.0 / (1.0 + jnp.exp(-SLOPE_FACTOR * (aerial - LEVEL_VALUE)))
        resist_rows[block * half : block * half + padded, :] = resist
        top = TARGET_HALO - margin + block * half
        target = pltpu.roll(target_rows[top : top + padded, :], width - margin, 1)
        sense = 2.0 * (resist - target) * SLOPE_FACTOR * resist * (1.0 - resist)
        clip_row = tile * rows - margin + block * half + row_at
        inside = jnp.logical_and(jnp.logical_and(clip_row >= 0, clip_row < clip_rows), row_at < half)
        sense = jnp.where(jnp.logical_and(inside, col_inside), sense, 0.0)
        for source in range(kern_count):
            scaled = (2.0 * shares[source]) * sense
            for part in range(2):
                first = (2 * source + part) * padded
                adjoint[first : first + padded, lanes] = (
                    scaled * fields[first : first + padded, lanes]
                ).astype(jnp.bfloat16)
    resist_out[...] = pltpu.roll(resist_rows[margin : margin + rows, :], width - margin, 1)[:, :share]

    spread[...] = lax.dot_general(
        toeplitz[...], adjoint[...], (((0,), (0,)), ((), ())), preferred_element_type=jnp.float32
    )

    grads = []
    for block in range(2):
        lanes = slice(block * width, (block + 1) * width)
        gathered = spread[0:PITCH, lanes]
        for column in range(1, span):
            place = slot_of(column) * PITCH
            gathered = gathered + pltpu.roll(spread[place : place + PITCH, lanes], column, 1)
        grads.append(gathered)
    grad_rows[...] = jnp.zeros_like(grad_rows)
    grad_rows[0:PITCH, :] = grads[0]
    grad_rows[half : half + PITCH, :] += grads[1]
    grad_out[...] = pltpu.roll(
        grad_rows[2 * margin : 2 * margin + rows, :], width - 2 * margin, 1
    )[:, :share]

    for copy in tap_copies:
        copy.wait_send()
    pl.when(has_up)(upward.wait_send)
    pl.when(has_down)(downward.wait_send)


def on_device(mask, target, kernels, source_weight, assign):
    rows, col_count = mask.shape
    span = kernels.shape[-1]
    margin = (span - 1) // 2
    kern_count = lax.axis_size("kern")
    tile_count = lax.axis_size("tile")
    share = col_count // kern_count
    width = -(-(share + 4 * margin) // 128) * 128
    depth = (span + span % 2) * PITCH
    half = (rows + 2 * margin) // 2
    padded = -(-half // 8) * 8
    parts = 2 * kern_count
    halo = MASK_HALO + TARGET_HALO
    in_hbm = pl.BlockSpec(memory_space=pl.ANY)
    return pl.pallas_call(
        functools.partial(gradient_kernel, (kern_count, tile_count, span, share, width)),
        out_shape=(
            jax.ShapeDtypeStruct((rows, share), jnp.float32),
            jax.ShapeDtypeStruct((rows, share), jnp.float32),
        ),
        in_specs=[in_hbm, in_hbm, IN_VMEM, IN_VMEM, pl.BlockSpec(memory_space=pltpu.SMEM)],
        out_specs=(IN_VMEM, IN_VMEM),
        scratch_shapes=[
            pltpu.VMEM((rows, width + 128), jnp.float32),
            pltpu.VMEM((rows, width + 128), jnp.int32),
            pltpu.VMEM((halo, width), jnp.bfloat16),
            pltpu.VMEM((halo, width), jnp.bfloat16),
            pltpu.VMEM((halo, width), jnp.bfloat16),
            pltpu.VMEM((halo, width), jnp.bfloat16),
            pltpu.VMEM((2, 128, 128), jnp.float32),
            pltpu.VMEM((16, 128), jnp.bfloat16),
            pltpu.VMEM((kern_count, 16, 128), jnp.bfloat16),
            pltpu.VMEM((rows + 2 * MASK_HALO, width), jnp.float32),
            pltpu.VMEM((rows + 2 * TARGET_HALO, width), jnp.float32),
            pltpu.VMEM((parts * padded, depth), jnp.bfloat16),
            pltpu.VMEM((depth, 2 * width), jnp.bfloat16),
            pltpu.VMEM((parts * padded, 2 * width), jnp.float32),
            pltpu.VMEM((parts * padded, 2 * width), jnp.bfloat16),
            pltpu.VMEM((depth, 2 * width), jnp.float32),
            pltpu.VMEM((half + padded, width), jnp.float32),
            pltpu.VMEM((half + PITCH, width), jnp.float32),
            pltpu.SemaphoreType.DMA((2,)),
            pltpu.SemaphoreType.DMA((kern_count,)),
            pltpu.SemaphoreType.DMA((kern_count,)),
            pltpu.SemaphoreType.DMA((2,)),
            pltpu.SemaphoreType.DMA((2,)),
        ],
        compiler_params=pltpu.CompilerParams(
            collective_id=0, has_side_effects=True, vmem_limit_bytes=56 * 1024 * 1024
        ),
        name="image_gradient",
    )(mask, target, jnp.swapaxes(kernels[0], 0, 1), source_weight[None, :], assign)


def solution(mesh):
    placed = (P("tile", None), P("tile", None), P("kern", None, None, None), P(), P("kern"))
    return jax.shard_map(
        on_device,
        mesh=mesh,
        in_specs=placed,
        out_specs=(P("tile", "kern"), P("tile", "kern")),
        check_vma=False,
    )
```

time: 24.6 us -> 19.4 us (0.79)
  the two profiles are of different devices: /device:TPU:0 before, /device:TPU:1 now
where the time goes in v2:
time: 19.4 us; the launch traced here: 19.2 us
  Pallas kernels  15.8 us (81%)
  local copies, waits for them, and re-layouts  2.14 us (11%)
  between operations  1.29 us (7%)
    pallas_call x1, Pallas kernels, on_device(): pl.pallas_call(functools.partial(gradient_kernel, (kern_count, tile_count...  15.8 us
    unnamed x4, local copies, waits for them, and re-layouts  2.14 us

profile of v2, /device:TPU:1, one launch (start us, length us, event | category | flops | bytes accessed | tf_op | source)
XLA Modules:
  0.0 19.2 jit_solution(10019754054783841485)
XLA Ops:
  1.3 15.8 %image_gradient.1 = (f32[64,256]{1,0:T(8,128)}, f32[64,256]{1,0:T(8,128)}) custom-call(f32[64,2048]{1,0:T(8,128)} %mask_hbm.1, s32[64,2048]{1,0:T(8,128)} %target_hbm.1, bf16[21,2,21]{2,1,0:T(2,128)(2,1)} %bitcast.4, f32[1,8]{1,0:T(1,128)} %bitcast.5, s32[1]{0:T(128)S(6)} %copy.9.assign_ref), custom_call_target="tpu_custom_call" | custom-call | tf_op jit(solution)/shard_map/image_gradient/pallas_call | solution.py:272
  17.0 0.0 copy-start
  17.1 1.5 %copy.10 = f32[64,256]{1,0:T(8,128)} copy(f32[64,256]{1,0:T(8,128)} %get-tuple-element.4) | data formatting | bytes 131072
  18.6 0.0 copy-done
  18.6 0.6 %copy.11 = f32[64,256]{1,0:T(8,128)} copy(f32[64,256]{1,0:T(8,128)S(1)} %copy-done) | data formatting | bytes 131072
Async XLA Ops:
  17.0 1.5 %copy-start = (f32[64,256]{1,0:T(8,128)S(1)}, f32[64,256]{1,0:T(8,128)}, u32[]{:S(2)}) copy-start(f32[64,256]{1,0:T(8,128)} %get-tuple-element.5) | copy-start | bytes 196612

commit v3 on v2

v3 whole, which is shorter than its diff:
```python
import functools

import jax
import jax.numpy as jnp
from jax import lax
from jax.experimental import pallas as pl
from jax.experimental.pallas import tpu as pltpu
from jax.sharding import PartitionSpec as P

SLOPE_FACTOR = 4.0
LEVEL_VALUE = 0.6
BLOCKS = 3
PITCH = 48
MASK_HALO = 32
TARGET_HALO = 16
MESH = pl.DeviceIdType.MESH
IN_VMEM = pl.BlockSpec(memory_space=pltpu.VMEM)
IN_ANY = pl.BlockSpec(memory_space=pl.ANY)


def gradient_kernel(
    sizes, mask_hbm, target_hbm, kernel_ref, weight_ref, assign_hbm, grad_out, resist_out,
    mask_window, target_window, send_up, send_down, above, below, square, tap_rows, own_taps,
    all_taps, mask_rows, target_rows, toeplitz, shifted, fields, adjoint, spread, resist_rows,
    grad_rows, resist_own, grad_own, assign_own, load_sem, store_sem, tap_send, tap_recv, halo_send, halo_recv,
):
    kern_count, tile_count, span, share, width = sizes
    tile = lax.axis_index("tile")
    kern = lax.axis_index("kern")
    rows, clip_cols = mask_hbm.shape
    clip_rows = rows * tile_count
    margin = (span - 1) // 2
    height = (rows + 2 * margin) // BLOCKS
    padded = -(-height // 16) * 16
    depth = toeplitz.shape[1]
    reach = share + 4 * margin
    lanes = shifted.shape[1]
    has_up = tile > 0
    has_down = tile < tile_count - 1

    barrier = pltpu.get_barrier_semaphore()
    for step in range(1, kern_count):
        peer = lax.rem(kern + step, kern_count)
        pl.semaphore_signal(barrier, inc=1, device_id=(tile, peer), device_id_type=MESH)

    @pl.when(has_up)
    def _():
        pl.semaphore_signal(barrier, inc=1, device_id=(tile - 1, kern), device_id_type=MESH)

    @pl.when(has_down)
    def _():
        pl.semaphore_signal(barrier, inc=1, device_id=(tile + 1, kern), device_id_type=MESH)

    start = kern * share - 2 * margin
    loaded = width + 128
    base = (start + 128) // 128 * 128 - 128
    base = jnp.minimum(jnp.maximum(base, 0), clip_cols - loaded)
    base = pl.multiple_of(base, 128)
    assign_load = pltpu.make_async_copy(assign_hbm, assign_own, load_sem.at[2])
    assign_load.start()
    loads = [
        pltpu.make_async_copy(mask_hbm.at[:, pl.ds(base, loaded)], mask_window, load_sem.at[0]),
        pltpu.make_async_copy(target_hbm.at[:, pl.ds(base, loaded)], target_window, load_sem.at[1]),
    ]
    for load in loads:
        load.start()

    square[...] = jnp.zeros_like(square)
    for row in range(span):
        pair = kernel_ref[row].astype(jnp.float32)
        square[0, row : row + 1, 0:span] = pair[0:1]
        square[1, row : row + 1, 0:span] = pair[1:2]
    assign_load.wait()
    lane = lax.broadcasted_iota(jnp.int32, (1, 128), 1)
    chunk_count = depth // 128
    for part in range(2):
        turned = square[part].T
        chunks = [jnp.zeros((1, 128), jnp.float32)] * chunk_count
        for column in range(span):
            chunk, offset = divmod(column * PITCH, 128)
            row = turned[column : column + 1]
            row = pltpu.roll(row, offset, 1) if offset else row
            if offset + span <= 128:
                chunks[chunk] = chunks[chunk] + row
            else:
                chunks[chunk] = chunks[chunk] + jnp.where(lane >= offset, row, 0.0)
                chunks[chunk + 1] = chunks[chunk + 1] + jnp.where(lane < offset, row, 0.0)
        mark = assign_own[0].astype(jnp.float32)
        chunks[-1] = jnp.where(lane >= 112, mark, chunks[-1])
        for chunk in range(chunk_count):
            tap_rows[8 * part + chunk : 8 * part + chunk + 1, :] = chunks[chunk]
    own_taps[...] = tap_rows[...].astype(jnp.bfloat16)

    pl.semaphore_wait(barrier, kern_count - 1 + has_up.astype(jnp.int32) + has_down.astype(jnp.int32))
    tap_copies = []
    for step in range(1, kern_count):
        peer = lax.rem(kern + step, kern_count)
        tap_copies.append(
            pltpu.make_async_remote_copy(
                src_ref=own_taps,
                dst_ref=all_taps.at[step],
                send_sem=tap_send.at[step],
                recv_sem=tap_recv.at[step],
                device_id=(tile, peer),
                device_id_type=MESH,
            )
        )
    for copy in tap_copies:
        copy.start()

    for load in loads:
        load.wait()
    clip_col = start + lax.broadcasted_iota(jnp.int32, (rows, width), 1)
    col_inside = jnp.logical_and(clip_col >= 0, clip_col < clip_cols)
    back = lax.rem(base - start + loaded, loaded)
    mask_own = pltpu.roll(mask_window[...], back, 1)[:, :width]
    mask_own = jnp.where(col_inside, mask_own, 0.0).astype(jnp.bfloat16)
    target_own = pltpu.roll(target_window[...].astype(jnp.float32), back, 1)[:, :width]
    target_own = target_own.astype(jnp.bfloat16)
    send_up[0:MASK_HALO, :] = mask_own[0:MASK_HALO]
    send_up[MASK_HALO:, :] = target_own[0:TARGET_HALO]
    send_down[0:MASK_HALO, :] = mask_own[rows - MASK_HALO :]
    send_down[MASK_HALO:, :] = target_own[rows - TARGET_HALO :]
    upward = pltpu.make_async_remote_copy(
        src_ref=send_up,
        dst_ref=below,
        send_sem=halo_send.at[0],
        recv_sem=halo_recv.at[0],
        device_id=(tile - 1, kern),
        device_id_type=MESH,
    )
    downward = pltpu.make_async_remote_copy(
        src_ref=send_down,
        dst_ref=above,
        send_sem=halo_send.at[1],
        recv_sem=halo_recv.at[1],
        device_id=(tile + 1, kern),
        device_id_type=MESH,
    )
    pl.when(has_up)(upward.start)
    pl.when(has_down)(downward.start)
    mask_rows[MASK_HALO : MASK_HALO + rows, :] = mask_own.astype(jnp.float32)
    target_rows[TARGET_HALO : TARGET_HALO + rows, :] = target_own.astype(jnp.float32)

    weights = weight_ref[...]
    total = jnp.sum(weights, axis=1, keepdims=True)
    slot_ids = lax.broadcasted_iota(jnp.int32, weights.shape, 1).astype(jnp.float32)
    own_lane = lax.broadcasted_iota(jnp.int32, (padded, 128), 1)
    own_row = lax.broadcasted_iota(jnp.int32, (padded, 128), 0)
    same_chunk = own_lane >= own_row
    shares = []
    for source in range(kern_count):
        if source == 0:
            block = own_taps[...].astype(jnp.float32)
        else:
            tap_copies[source - 1].wait_recv()
            block = all_taps[source].astype(jnp.float32)
        picked = jnp.where(slot_ids == block[7:8, 112:113], weights, 0.0)
        shares.append(jnp.sum(picked, axis=1, keepdims=True) / total)
        for part in range(2):
            first = (2 * source + part) * padded
            before = jnp.zeros((padded, 128), jnp.float32)
            for chunk in range(chunk_count):
                at = 8 * part + chunk
                row = jnp.broadcast_to(block[at : at + 1], (padded, 128))
                turned = pltpu.roll(row, 0, 1, stride=1, stride_axis=0)
                toeplitz[first : first + padded, chunk * 128 : (chunk + 1) * 128] = jnp.where(
                    same_chunk, turned, before
                ).astype(jnp.bfloat16)
                before = turned

    @pl.when(has_up)
    def _():
        downward.wait_recv()

    @pl.when(jnp.logical_not(has_up))
    def _():
        above[...] = jnp.zeros_like(above)

    @pl.when(has_down)
    def _():
        upward.wait_recv()

    @pl.when(jnp.logical_not(has_down))
    def _():
        below[...] = jnp.zeros_like(below)

    mask_rows[0:MASK_HALO, :] = above[0:MASK_HALO, :].astype(jnp.float32)
    mask_rows[MASK_HALO + rows :, :] = below[0:MASK_HALO, :].astype(jnp.float32)
    target_rows[0:TARGET_HALO, :] = above[MASK_HALO:, :].astype(jnp.float32)
    target_rows[TARGET_HALO + rows :, :] = below[MASK_HALO:, :].astype(jnp.float32)

    def side_by_side(held, top, count, shift):
        pieces = []
        for block in range(BLOCKS):
            piece = held[top + block * height : top + block * height + count, :]
            piece = pltpu.roll(piece, width - shift, 1) if shift else piece
            pieces.append(piece[:, :reach])
        if lanes > BLOCKS * reach:
            pieces.append(jnp.zeros((count, lanes - BLOCKS * reach), jnp.float32))
        return jnp.concatenate(pieces, axis=1)

    window = side_by_side(mask_rows, MASK_HALO - 2 * margin, PITCH, 0)
    for column in range(span):
        turned = window if column == 0 else pltpu.roll(window, lanes - column, 1)
        shifted[column * PITCH : (column + 1) * PITCH, :] = turned.astype(jnp.bfloat16)
    shifted[span * PITCH :, :] = jnp.zeros((depth - span * PITCH, lanes), jnp.bfloat16)

    fields[...] = jnp.dot(toeplitz[...], shifted[...], preferred_element_type=jnp.float32)

    row_at = lax.broadcasted_iota(jnp.int32, (padded, lanes), 0)
    col_at = lax.broadcasted_iota(jnp.int32, (padded, lanes), 1)
    clip_row = tile * rows - margin + row_at
    clip_col = kern * share - margin + col_at
    for block in range(1, BLOCKS):
        later = col_at >= block * reach
        clip_row = jnp.where(later, clip_row + height, clip_row)
        clip_col = jnp.where(later, clip_col - reach, clip_col)
    inside = jnp.logical_and(
        jnp.logical_and(clip_row >= 0, clip_row < clip_rows),
        jnp.logical_and(clip_col >= 0, clip_col < clip_cols),
    )
    inside = jnp.logical_and(inside, row_at < height)
    target = side_by_side(target_rows, TARGET_HALO - margin, padded, margin)
    aerial = jnp.zeros((padded, lanes), jnp.float32)
    for source in range(kern_count):
        first = 2 * source * padded
        real = fields[first : first + padded, :]
        imag = fields[first + padded : first + 2 * padded, :]
        aerial = aerial + shares[source] * (real * real + imag * imag)
    resist = 1.0 / (1.0 + jnp.exp(-SLOPE_FACTOR * (aerial - LEVEL_VALUE)))
    sense = 2.0 * (resist - target) * SLOPE_FACTOR * resist * (1.0 - resist)
    sense = jnp.where(inside, sense, 0.0)
    for source in range(kern_count):
        scaled = (2.0 * shares[source]) * sense
        for part in range(2):
            first = (2 * source + part) * padded
            adjoint[first : first + padded, :] = (
                scaled * fields[first : first + padded, :]
            ).astype(jnp.bfloat16)
    for block in range(BLOCKS):
        piece = pltpu.roll(resist, lanes - block * reach - margin, 1)[:, :share]
        resist_rows[block * height : block * height + padded, :] = piece
    resist_own[...] = resist_rows[margin : margin + rows, :]
    resist_store = pltpu.make_async_copy(resist_own, resist_out, store_sem.at[0])
    resist_store.start()

    spread[...] = lax.dot_general(
        toeplitz[...], adjoint[...], (((0,), (0,)), ((), ())), preferred_element_type=jnp.float32
    )

    gathered = spread[0:PITCH, :]
    for column in range(1, span):
        place = column * PITCH
        gathered = gathered + pltpu.roll(spread[place : place + PITCH, :], column, 1)
    grad_rows[...] = jnp.zeros_like(grad_rows)
    for block in range(BLOCKS):
        piece = pltpu.roll(gathered, lanes - block * reach - 2 * margin, 1)[:, :share]
        grad_rows[block * height : block * height + PITCH, :] += piece
    grad_own[...] = grad_rows[2 * margin : 2 * margin + rows, :]
    grad_store = pltpu.make_async_copy(grad_own, grad_out, store_sem.at[1])
    grad_store.start()

    for copy in tap_copies:
        copy.wait_send()
    pl.when(has_up)(upward.wait_send)
    pl.when(has_down)(downward.wait_send)
    resist_store.wait()
    grad_store.wait()


def hand_over_kernel(grad_in, resist_in, grad_out, resist_out, sems):
    moves = [
        pltpu.make_async_copy(grad_in, grad_out, sems.at[0]),
        pltpu.make_async_copy(resist_in, resist_out, sems.at[1]),
    ]
    for move in moves:
        move.start()
    for move in moves:
        move.wait()


def on_device(mask, target, kernels, source_weight, assign):
    rows, col_count = mask.shape
    span = kernels.shape[-1]
    margin = (span - 1) // 2
    kern_count = lax.axis_size("kern")
    tile_count = lax.axis_size("tile")
    share = col_count // kern_count
    reach = share + 4 * margin
    width = -(-reach // 128) * 128
    lanes = -(-BLOCKS * reach // 128) * 128
    depth = -(-span * PITCH // 128) * 128
    height = (rows + 2 * margin) // BLOCKS
    padded = -(-height // 16) * 16
    parts = 2 * kern_count
    halo = MASK_HALO + TARGET_HALO
    image = jax.ShapeDtypeStruct((rows, share), jnp.float32)
    images = pl.pallas_call(
        functools.partial(gradient_kernel, (kern_count, tile_count, span, share, width)),
        out_shape=(image, image),
        in_specs=[IN_ANY, IN_ANY, IN_VMEM, IN_VMEM, IN_ANY],
        out_specs=(IN_ANY, IN_ANY),
        scratch_shapes=[
            pltpu.VMEM((rows, width + 128), jnp.float32),
            pltpu.VMEM((rows, width + 128), jnp.int32),
            pltpu.VMEM((halo, width), jnp.bfloat16),
            pltpu.VMEM((halo, width), jnp.bfloat16),
            pltpu.VMEM((halo, width), jnp.bfloat16),
            pltpu.VMEM((halo, width), jnp.bfloat16),
            pltpu.VMEM((2, 128, 128), jnp.float32),
            pltpu.VMEM((16, 128), jnp.float32),
            pltpu.VMEM((16, 128), jnp.bfloat16),
            pltpu.VMEM((kern_count, 16, 128), jnp.bfloat16),
            pltpu.VMEM((rows + 2 * MASK_HALO, width), jnp.float32),
            pltpu.VMEM((rows + 2 * TARGET_HALO, width), jnp.float32),
            pltpu.VMEM((parts * padded, depth), jnp.bfloat16),
            pltpu.VMEM((depth, lanes), jnp.bfloat16),
            pltpu.VMEM((parts * padded, lanes), jnp.float32),
            pltpu.VMEM((parts * padded, lanes), jnp.bfloat16),
            pltpu.VMEM((depth, lanes), jnp.float32),
            pltpu.VMEM(((BLOCKS - 1) * height + padded, share), jnp.float32),
            pltpu.VMEM(((BLOCKS - 1) * height + PITCH, share), jnp.float32),
            pltpu.VMEM((rows, share), jnp.float32),
            pltpu.VMEM((rows, share), jnp.float32),
            pltpu.SMEM((1,), jnp.int32),
            pltpu.SemaphoreType.DMA((3,)),
            pltpu.SemaphoreType.DMA((2,)),
            pltpu.SemaphoreType.DMA((kern_count,)),
            pltpu.SemaphoreType.DMA((kern_count,)),
            pltpu.SemaphoreType.DMA((2,)),
            pltpu.SemaphoreType.DMA((2,)),
        ],
        compiler_params=pltpu.CompilerParams(
            collective_id=0, has_side_effects=True, vmem_limit_bytes=56 * 1024 * 1024
        ),
        name="image_gradient",
    )(mask, target, jnp.swapaxes(kernels[0], 0, 1), source_weight[None, :], assign)
    return pl.pallas_call(
        hand_over_kernel,
        out_shape=(image, image),
        in_specs=[IN_ANY, IN_ANY],
        out_specs=(IN_ANY, IN_ANY),
        scratch_shapes=[pltpu.SemaphoreType.DMA((2,))],
        compiler_params=pltpu.CompilerParams(vmem_limit_bytes=56 * 1024 * 1024),
        name="hand_over",
    )(*images)


def solution(mesh):
    placed = (P("tile", None), P("tile", None), P("kern", None, None, None), P(), P("kern"))
    return jax.shard_map(
        on_device,
        mesh=mesh,
        in_specs=placed,
        out_specs=(P("tile", "kern"), P("tile", "kern")),
        check_vma=False,
    )
```

time: 19.4 us -> 20.6 us (1.062)
  the two profiles are of different devices: /device:TPU:1 before, /device:TPU:0 now
where the time goes in v3:
time: 20.6 us; the launch traced here: 20.4 us
  Pallas kernels  19.1 us (93%)
  between operations  1.29 us (6%)
    pallas_call x1, Pallas kernels, on_device(): pl.pallas_call(functools.partial(gradient_kernel, (kern_count, tile_count...  14 us
    pallas_call x1, Pallas kernels, on_device(): pl.pallas_call(hand_over_kernel, out_shape=(image, image), in_specs=[IN_A...  5.09 us

profile of v3, /device:TPU:0, one launch (start us, length us, event | category | flops | bytes accessed | tf_op | source)
XLA Modules:
  0.0 20.4 jit_solution(10196825215677036791)
XLA Ops:
  1.3 14.0 %image_gradient.1 = (f32[64,256]{1,0:T(8,128)}, f32[64,256]{1,0:T(8,128)}) custom-call(f32[64,2048]{1,0:T(8,128)} %mask_hbm.1, s32[64,2048]{1,0:T(8,128)} %target_hbm.1, bf16[21,2,21]{2,1,0:T(2,128)(2,1)} %bitcast.4, f32[1,8]{1,0:T(1,128)} %bitcast.5, s32[1]{0:T(128)S(6)} %copy.7.assign_hbm), custom_call_target="tpu_custom_call" | custom-call | tf_op jit(solution)/shard_map/image_gradient/pallas_call | solution.py:299
  15.3 5.1 %hand_over.1 = (f32[64,256]{1,0:T(8,128)}, f32[64,256]{1,0:T(8,128)}) custom-call(f32[64,256]{1,0:T(8,128)} %get-tuple-element.4.grad_in, f32[64,256]{1,0:T(8,128)} %get-tuple-element.5.resist_in), custom_call_target="tpu_custom_call" | custom-call | tf_op jit(solution)/shard_map/hand_over/pallas_call | solution.py:339

commit v4 on v3

--- a/solution.py
+++ b/solution.py
@@ -19,10 +19,10 @@
 
 
 def gradient_kernel(
-    sizes, mask_hbm, target_hbm, kernel_ref, weight_ref, assign_hbm, grad_out, resist_out,
+    sizes, mask_hbm, target_hbm, kernel_hbm, weight_hbm, assign_hbm, grad_out, resist_out,
     mask_window, target_window, send_up, send_down, above, below, square, tap_rows, own_taps,
     all_taps, mask_rows, target_rows, toeplitz, shifted, fields, adjoint, spread, resist_rows,
-    grad_rows, resist_own, grad_own, assign_own, load_sem, store_sem, tap_send, tap_recv, halo_send, halo_recv,
+    grad_rows, resist_own, grad_own, kernel_ref, weight_ref, assign_own, load_sem, store_sem, tap_send, tap_recv, halo_send, halo_recv,
 ):
     kern_count, tile_count, span, share, width = sizes
     tile = lax.axis_index("tile")
@@ -56,8 +56,13 @@
     base = (start + 128) // 128 * 128 - 128
     base = jnp.minimum(jnp.maximum(base, 0), clip_cols - loaded)
     base = pl.multiple_of(base, 128)
-    assign_load = pltpu.make_async_copy(assign_hbm, assign_own, load_sem.at[2])
-    assign_load.start()
+    small_loads = [
+        pltpu.make_async_copy(kernel_hbm, kernel_ref, load_sem.at[2]),
+        pltpu.make_async_copy(weight_hbm, weight_ref, load_sem.at[3]),
+        pltpu.make_async_copy(assign_hbm, assign_own, load_sem.at[4]),
+    ]
+    for load in small_loads:
+        load.start()
     loads = [
         pltpu.make_async_copy(mask_hbm.at[:, pl.ds(base, loaded)], mask_window, load_sem.at[0]),
         pltpu.make_async_copy(target_hbm.at[:, pl.ds(base, loaded)], target_window, load_sem.at[1]),
@@ -66,11 +71,12 @@
         load.start()
 
     square[...] = jnp.zeros_like(square)
+    for load in small_loads:
+        load.wait()
     for row in range(span):
         pair = kernel_ref[row].astype(jnp.float32)
         square[0, row : row + 1, 0:span] = pair[0:1]
         square[1, row : row + 1, 0:span] = pair[1:2]
-    assign_load.wait()
     lane = lax.broadcasted_iota(jnp.int32, (1, 128), 1)
     chunk_count = depth // 128
     for part in range(2):
@@ -90,23 +96,6 @@
         for chunk in range(chunk_count):
             tap_rows[8 * part + chunk : 8 * part + chunk + 1, :] = chunks[chunk]
     own_taps[...] = tap_rows[...].astype(jnp.bfloat16)
-
-    pl.semaphore_wait(barrier, kern_count - 1 + has_up.astype(jnp.int32) + has_down.astype(jnp.int32))
-    tap_copies = []
-    for step in range(1, kern_count):
-        peer = lax.rem(kern + step, kern_count)
-        tap_copies.append(
-            pltpu.make_async_remote_copy(
-                src_ref=own_taps,
-                dst_ref=all_taps.at[step],
-                send_sem=tap_send.at[step],
-                recv_sem=tap_recv.at[step],
-                device_id=(tile, peer),
-                device_id_type=MESH,
-            )
-        )
-    for copy in tap_copies:
-        copy.start()
 
     for load in loads:
         load.wait()
@@ -137,10 +126,63 @@
         device_id=(tile + 1, kern),
         device_id_type=MESH,
     )
+    pl.semaphore_wait(barrier, kern_count - 1 + has_up.astype(jnp.int32) + has_down.astype(jnp.int32))
+    tap_copies = []
+    for step in range(1, kern_count):
+        peer = lax.rem(kern + step, kern_count)
+        tap_copies.append(
+            pltpu.make_async_remote_copy(
+                src_ref=own_taps,
+                dst_ref=all_taps.at[step],
+                send_sem=tap_send.at[step],
+                recv_sem=tap_recv.at[step],
+                device_id=(tile, peer),
+                device_id_type=MESH,
+            )
+        )
+    for copy in tap_copies:
+        copy.start()
     pl.when(has_up)(upward.start)
     pl.when(has_down)(downward.start)
     mask_rows[MASK_HALO : MASK_HALO + rows, :] = mask_own.astype(jnp.float32)
     target_rows[TARGET_HALO : TARGET_HALO + rows, :] = target_own.astype(jnp.float32)
+
+    @pl.when(has_up)
+    def _():
+        downward.wait_recv()
+
+    @pl.when(jnp.logical_not(has_up))
+    def _():
+        above[...] = jnp.zeros_like(above)
+
+    @pl.when(has_down)
+    def _():
+        upward.wait_recv()
+
+    @pl.when(jnp.logical_not(has_down))
+    def _():
+        below[...] = jnp.zeros_like(below)
+
+    mask_rows[0:MASK_HALO, :] = above[0:MASK_HALO, :].astype(jnp.float32)
+    mask_rows[MASK_HALO + rows :, :] = below[0:MASK_HALO, :].astype(jnp.float32)
+    target_rows[0:TARGET_HALO, :] = above[MASK_HALO:, :].astype(jnp.float32)
+    target_rows[TARGET_HALO + rows :, :] = below[MASK_HALO:, :].astype(jnp.float32)
+
+    def side_by_side(held, top, count, shift):
+        pieces = []
+        for block in range(BLOCKS):
+            piece = held[top + block * height : top + block * height + count, :]
+            piece = pltpu.roll(piece, width - shift, 1) if shift else piece
+            pieces.append(piece[:, :reach])
+        if lanes > BLOCKS * reach:
+            pieces.append(jnp.zeros((count, lanes - BLOCKS * reach), jnp.float32))
+        return jnp.concatenate(pieces, axis=1)
+
+    window = side_by_side(mask_rows, MASK_HALO - 2 * margin, PITCH, 0)
+    for column in range(span):
+        turned = window if column == 0 else pltpu.roll(window, lanes - column, 1)
+        shifted[column * PITCH : (column + 1) * PITCH, :] = turned.astype(jnp.bfloat16)
+    shifted[span * PITCH :, :] = jnp.zeros((depth - span * PITCH, lanes), jnp.bfloat16)
 
     weights = weight_ref[...]
     total = jnp.sum(weights, axis=1, keepdims=True)
@@ -169,43 +211,6 @@
                 ).astype(jnp.bfloat16)
                 before = turned
 
-    @pl.when(has_up)
-    def _():
-        downward.wait_recv()
-
-    @pl.when(jnp.logical_not(has_up))
-    def _():
-        above[...] = jnp.zeros_like(above)
-
-    @pl.when(has_down)
-    def _():
-        upward.wait_recv()
-
-    @pl.when(jnp.logical_not(has_down))
-    def _():
-        below[...] = jnp.zeros_like(below)
-
-    mask_rows[0:MASK_HALO, :] = above[0:MASK_HALO, :].astype(jnp.float32)
-    mask_rows[MASK_HALO + rows :, :] = below[0:MASK_HALO, :].astype(jnp.float32)
-    target_rows[0:TARGET_HALO, :] = above[MASK_HALO:, :].astype(jnp.float32)
-    target_rows[TARGET_HALO + rows :, :] = below[MASK_HALO:, :].astype(jnp.float32)
-
-    def side_by_side(held, top, count, shift):
-        pieces = []
-        for block in range(BLOCKS):
-            piece = held[top + block * height : top + block * height + count, :]
-            piece = pltpu.roll(piece, width - shift, 1) if shift else piece
-            pieces.append(piece[:, :reach])
-        if lanes > BLOCKS * reach:
-            pieces.append(jnp.zeros((count, lanes - BLOCKS * reach), jnp.float32))
-        return jnp.concatenate(pieces, axis=1)
-
-    window = side_by_side(mask_rows, MASK_HALO - 2 * margin, PITCH, 0)
-    for column in range(span):
-        turned = window if column == 0 else pltpu.roll(window, lanes - column, 1)
-        shifted[column * PITCH : (column + 1) * PITCH, :] = turned.astype(jnp.bfloat16)
-    shifted[span * PITCH :, :] = jnp.zeros((depth - span * PITCH, lanes), jnp.bfloat16)
-
     fields[...] = jnp.dot(toeplitz[...], shifted[...], preferred_element_type=jnp.float32)
 
     row_at = lax.broadcasted_iota(jnp.int32, (padded, lanes), 0)
@@ -269,15 +274,19 @@
     grad_store.wait()
 
 
-def hand_over_kernel(grad_in, resist_in, grad_out, resist_out, sems):
-    moves = [
-        pltpu.make_async_copy(grad_in, grad_out, sems.at[0]),
-        pltpu.make_async_copy(resist_in, resist_out, sems.at[1]),
-    ]
-    for move in moves:
-        move.start()
-    for move in moves:
-        move.wait()
+def hand_over_kernel(grad_in, resist_in, grad_out, resist_out, held, sems):
+    images = ((grad_in, grad_out), (resist_in, resist_out))
+    loads, stores = [], []
+    for at, (taken, given) in enumerate(images):
+        loads.append(pltpu.make_async_copy(taken, held.at[at], sems.at[at]))
+        stores.append(pltpu.make_async_copy(held.at[at], given, sems.at[2 + at]))
+    for load in loads:
+        load.start()
+    for load, store in zip(loads, stores):
+        load.wait()
+        store.start()
+    for store in stores:
+        store.wait()
 
 
 def on_device(mask, target, kernels, source_weight, assign):
@@ -299,7 +308,7 @@
     images = pl.pallas_call(
         functools.partial(gradient_kernel, (kern_count, tile_count, span, share, width)),
         out_shape=(image, image),
-        in_specs=[IN_ANY, IN_ANY, IN_VMEM, IN_VMEM, IN_ANY],
+        in_specs=[IN_ANY] * 5,
         out_specs=(IN_ANY, IN_ANY),
         scratch_shapes=[
             pltpu.VMEM((rows, width + 128), jnp.float32),
@@ -323,8 +332,10 @@
             pltpu.VMEM(((BLOCKS - 1) * height + PITCH, share), jnp.float32),
             pltpu.VMEM((rows, share), jnp.float32),
             pltpu.VMEM((rows, share), jnp.float32),
+            pltpu.VMEM(kernels.shape[2:3] + kernels.shape[1:2] + kernels.shape[3:], kernels.dtype),
+            pltpu.VMEM((1, source_weight.shape[0]), jnp.float32),
             pltpu.SMEM((1,), jnp.int32),
-            pltpu.SemaphoreType.DMA((3,)),
+            pltpu.SemaphoreType.DMA((5,)),
             pltpu.SemaphoreType.DMA((2,)),
             pltpu.SemaphoreType.DMA((kern_count,)),
             pltpu.SemaphoreType.DMA((kern_count,)),
@@ -341,7 +352,10 @@
         out_shape=(image, image),
         in_specs=[IN_ANY, IN_ANY],
         out_specs=(IN_ANY, IN_ANY),
-        scratch_shapes=[pltpu.SemaphoreType.DMA((2,))],
+        scratch_shapes=[
+            pltpu.VMEM((2, rows, share), jnp.float32),
+            pltpu.SemaphoreType.DMA((4,)),
+        ],
         compiler_params=pltpu.CompilerParams(vmem_limit_bytes=56 * 1024 * 1024),
         name="hand_over",
     )(*images)

time: 20.6 us -> 17.1 us (0.83)
  the two profiles are of different devices: /device:TPU:0 before, /device:TPU:1 now
where the time goes in v4:
time: 17.1 us; the launch traced here: 16.9 us
  Pallas kernels  15.6 us (91%)
  between operations  1.29 us (8%)
    pallas_call x1, Pallas kernels, on_device(): pl.pallas_call(functools.partial(gradient_kernel, (kern_count, tile_count...  14.1 us
    pallas_call x1, Pallas kernels, on_device(): pl.pallas_call(hand_over_kernel, out_shape=(image, image), in_specs=[IN_A...  1.53 us

profile of v4, /device:TPU:1, one launch (start us, length us, event | category | flops | bytes accessed | tf_op | source)
XLA Modules:
  0.0 16.9 jit_solution(15666133731676873087)
XLA Ops:
  1.3 14.1 %image_gradient.1 = (f32[64,256]{1,0:T(8,128)}, f32[64,256]{1,0:T(8,128)}) custom-call(f32[64,2048]{1,0:T(8,128)} %mask_hbm.1, s32[64,2048]{1,0:T(8,128)} %target_hbm.1, bf16[21,2,21]{2,1,0:T(2,128)(2,1)} %bitcast.4, f32[1,8]{1,0:T(1,128)} %bitcast.5, s32[1]{0:T(128)S(6)} %copy.7.assign_hbm), custom_call_target="tpu_custom_call" | custom-call | tf_op jit(solution)/shard_map/image_gradient/pallas_call | solution.py:308
  15.3 1.5 %hand_over.1 = (f32[64,256]{1,0:T(8,128)}, f32[64,256]{1,0:T(8,128)}) custom-call(f32[64,256]{1,0:T(8,128)} %get-tuple-element.4.grad_in, f32[64,256]{1,0:T(8,128)} %get-tuple-element.5.resist_in), custom_call_target="tpu_custom_call" | custom-call | tf_op jit(solution)/shard_map/hand_over/pallas_call | solution.py:350

commit v5 on v4

--- a/solution.py
+++ b/solution.py
@@ -22,7 +22,7 @@
     sizes, mask_hbm, target_hbm, kernel_hbm, weight_hbm, assign_hbm, grad_out, resist_out,
     mask_window, target_window, send_up, send_down, above, below, square, tap_rows, own_taps,
     all_taps, mask_rows, target_rows, toeplitz, shifted, fields, adjoint, spread, resist_rows,
-    grad_rows, resist_own, grad_own, kernel_ref, weight_ref, assign_own, load_sem, store_sem, tap_send, tap_recv, halo_send, halo_recv,
+    grad_rows, kernel_ref, weight_ref, assign_own, load_sem, tap_send, tap_recv, halo_send, halo_recv,
 ):
     kern_count, tile_count, span, share, width = sizes
     tile = lax.axis_index("tile")
@@ -246,9 +246,7 @@
     for block in range(BLOCKS):
         piece = pltpu.roll(resist, lanes - block * reach - margin, 1)[:, :share]
         resist_rows[block * height : block * height + padded, :] = piece
-    resist_own[...] = resist_rows[margin : margin + rows, :]
-    resist_store = pltpu.make_async_copy(resist_own, resist_out, store_sem.at[0])
-    resist_store.start()
+    resist_out[...] = resist_rows[margin : margin + rows, :]
 
     spread[...] = lax.dot_general(
         toeplitz[...], adjoint[...], (((0,), (0,)), ((), ())), preferred_element_type=jnp.float32
@@ -262,31 +260,23 @@
     for block in range(BLOCKS):
         piece = pltpu.roll(gathered, lanes - block * reach - 2 * margin, 1)[:, :share]
         grad_rows[block * height : block * height + PITCH, :] += piece
-    grad_own[...] = grad_rows[2 * margin : 2 * margin + rows, :]
-    grad_store = pltpu.make_async_copy(grad_own, grad_out, store_sem.at[1])
-    grad_store.start()
+    grad_out[...] = grad_rows[2 * margin : 2 * margin + rows, :]
 
     for copy in tap_copies:
         copy.wait_send()
     pl.when(has_up)(upward.wait_send)
     pl.when(has_down)(downward.wait_send)
-    resist_store.wait()
-    grad_store.wait()
-
-
-def hand_over_kernel(grad_in, resist_in, grad_out, resist_out, held, sems):
-    images = ((grad_in, grad_out), (resist_in, resist_out))
-    loads, stores = [], []
-    for at, (taken, given) in enumerate(images):
-        loads.append(pltpu.make_async_copy(taken, held.at[at], sems.at[at]))
-        stores.append(pltpu.make_async_copy(held.at[at], given, sems.at[2 + at]))
-    for load in loads:
-        load.start()
-    for load, store in zip(loads, stores):
-        load.wait()
-        store.start()
-    for store in stores:
-        store.wait()
+
+
+def hand_over_kernel(grad_in, resist_in, grad_out, resist_out, sems):
+    moves = [
+        pltpu.make_async_copy(grad_in, grad_out, sems.at[0]),
+        pltpu.make_async_copy(resist_in, resist_out, sems.at[1]),
+    ]
+    for move in moves:
+        move.start()
+    for move in moves:
+        move.wait()
 
 
 def on_device(mask, target, kernels, source_weight, assign):
@@ -309,7 +299,7 @@
         functools.partial(gradient_kernel, (kern_count, tile_count, span, share, width)),
         out_shape=(image, image),
         in_specs=[IN_ANY] * 5,
-        out_specs=(IN_ANY, IN_ANY),
+        out_specs=(IN_VMEM, IN_VMEM),
         scratch_shapes=[
             pltpu.VMEM((rows, width + 128), jnp.float32),
             pltpu.VMEM((rows, width + 128), jnp.int32),
@@ -330,33 +320,27 @@
             pltpu.VMEM((depth, lanes), jnp.float32),
             pltpu.VMEM(((BLOCKS - 1) * height + padded, share), jnp.float32),
             pltpu.VMEM(((BLOCKS - 1) * height + PITCH, share), jnp.float32),
-            pltpu.VMEM((rows, share), jnp.float32),
-            pltpu.VMEM((rows, share), jnp.float32),
             pltpu.VMEM(kernels.shape[2:3] + kernels.shape[1:2] + kernels.shape[3:], kernels.dtype),
             pltpu.VMEM((1, source_weight.shape[0]), jnp.float32),
             pltpu.SMEM((1,), jnp.int32),
             pltpu.SemaphoreType.DMA((5,)),
-            pltpu.SemaphoreType.DMA((2,)),
             pltpu.SemaphoreType.DMA((kern_count,)),
             pltpu.SemaphoreType.DMA((kern_count,)),
             pltpu.SemaphoreType.DMA((2,)),
             pltpu.SemaphoreType.DMA((2,)),
         ],
         compiler_params=pltpu.CompilerParams(
-            collective_id=0, has_side_effects=True, vmem_limit_bytes=56 * 1024 * 1024
+            collective_id=0, has_side_effects=True, vmem_limit_bytes=55040 * 1024
         ),
         name="image_gradient",
     )(mask, target, jnp.swapaxes(kernels[0], 0, 1), source_weight[None, :], assign)
     return pl.pallas_call(
         hand_over_kernel,
         out_shape=(image, image),
-        in_specs=[IN_ANY, IN_ANY],
+        in_specs=[IN_VMEM, IN_VMEM],
         out_specs=(IN_ANY, IN_ANY),
-        scratch_shapes=[
-            pltpu.VMEM((2, rows, share), jnp.float32),
-            pltpu.SemaphoreType.DMA((4,)),
-        ],
-        compiler_params=pltpu.CompilerParams(vmem_limit_bytes=56 * 1024 * 1024),
+        scratch_shapes=[pltpu.SemaphoreType.DMA((2,))],
+        compiler_params=pltpu.CompilerParams(vmem_limit_bytes=1024 * 1024),
         name="hand_over",
     )(*images)
 

time: 17.1 us -> 17 us (level)
  Pallas kernels: 15.6 us -> 14.1 us
  local copies, waits for them, and re-layouts: 0 us -> 1.35 us
    unnamed x0 -> x4, local copies, waits for them, and re-layouts: none -> 1.35 us
    pallas_call x1, Pallas kernels: 1.53 us -> 0.67 us  [on_device(): pl.pallas_call(hand_over_kernel, out_shape=(image, image), in_specs=[IN_V...]
    pallas_call x1, Pallas kernels: 14.1 us -> 13.4 us  [on_device(): pl.pallas_call(functools.partial(gradient_kernel, (kern_count, tile_count...]
where the time goes in v5:
time: 17 us; the launch traced here: 16.7 us
  Pallas kernels  14.1 us (83%)
  local copies, waits for them, and re-layouts  1.35 us (8%)
  between operations  1.29 us (8%)
    pallas_call x1, Pallas kernels, on_device(): pl.pallas_call(functools.partial(gradient_kernel, (kern_count, tile_count...  13.4 us
    unnamed x4, local copies, waits for them, and re-layouts  1.35 us
    pallas_call x1, Pallas kernels, on_device(): pl.pallas_call(hand_over_kernel, out_shape=(image, image), in_specs=[IN_V...  0.67 us

profile of v5, /device:TPU:1, one launch (start us, length us, event | category | flops | bytes accessed | tf_op | source)
XLA Modules:
  0.0 16.7 jit_solution(139283081053490841)
XLA Ops:
  1.3 0.0 copy-start.1
  1.3 0.6 %copy-done.1 = f32[8]{0:T(128)S(1)} copy-done((f32[8]{0:T(128)S(1)}, f32[8]{0:T(128)}, u32[]{:S(2)}) %copy-start.1) | copy-done | bytes 56
  1.9 0.0 copy-start
  1.9 0.7 %copy-done = bf16[1,2,21,21]{3,1,2,0:T(2,128)(2,1)S(1)} copy-done((bf16[1,2,21,21]{3,1,2,0:T(2,128)(2,1)S(1)}, bf16[1,2,21,21]{3,1,2,0:T(2,128)(2,1)}, u32[]{:S(2)}) %copy-start) | copy-done | bytes 1788
  2.6 13.4 %image_gradient.1 = (f32[64,256]{1,0:T(8,128)S(1)}, f32[64,256]{1,0:T(8,128)S(1)}) custom-call(f32[64,2048]{1,0:T(8,128)} %mask_hbm.1, s32[64,2048]{1,0:T(8,128)} %target_hbm.1, bf16[21,2,21]{2,1,0:T(2,128)(2,1)S(1)} %bitcast.4, f32[1,8]{1,0:T(1,128)S(1)} %bitcast.5, s32[1]{0:T(128)S(6)} %copy.7.assign_hbm), custom_call_target="tpu_custom_call" | custom-call | tf_op jit(solution)/shard_map/image_gradient/pallas_call | solution.py:298
  16.1 0.7 %hand_over.1 = (f32[64,256]{1,0:T(8,128)}, f32[64,256]{1,0:T(8,128)}) custom-call(f32[64,256]{1,0:T(8,128)S(1)} %get-tuple-element.4.grad_in, f32[64,256]{1,0:T(8,128)S(1)} %get-tuple-element.5.resist_in), custom_call_target="tpu_custom_call" | custom-call | tf_op jit(solution)/shard_map/hand_over/pallas_call | solution.py:337
Async XLA Ops:
  1.3 0.7 %copy-start.1 = (f32[8]{0:T(128)S(1)}, f32[8]{0:T(128)}, u32[]{:S(2)}) copy-start(f32[8]{0:T(128)} %param.8) | copy-start | bytes 100
  1.9 0.7 %copy-start = (bf16[1,2,21,21]{3,1,2,0:T(2,128)(2,1)S(1)}, bf16[1,2,21,21]{3,1,2,0:T(2,128)(2,1)}, u32[]{:S(2)}) copy-start(bf16[1,2,21,21]{3,1,2,0:T(2,128)(2,1)} %param.7) | copy-start | bytes 5296

commit v6 on v4

--- a/solution.py
+++ b/solution.py
@@ -18,23 +18,44 @@
 IN_ANY = pl.BlockSpec(memory_space=pl.ANY)
 
 
-def gradient_kernel(
-    sizes, mask_hbm, target_hbm, kernel_hbm, weight_hbm, assign_hbm, grad_out, resist_out,
-    mask_window, target_window, send_up, send_down, above, below, square, tap_rows, own_taps,
-    all_taps, mask_rows, target_rows, toeplitz, shifted, fields, adjoint, spread, resist_rows,
-    grad_rows, resist_own, grad_own, kernel_ref, weight_ref, assign_own, load_sem, store_sem, tap_send, tap_recv, halo_send, halo_recv,
+def window_of(mask_hbm, target_hbm, mask_window, target_window, sems, share, margin):
+    rows, clip_cols = mask_hbm.shape
+    loaded = mask_window.shape[1]
+    width = loaded - 128
+    start = lax.axis_index("kern") * share - 2 * margin
+    base = (start + 128) // 128 * 128 - 128
+    base = jnp.minimum(jnp.maximum(base, 0), clip_cols - loaded)
+    base = pl.multiple_of(base, 128)
+    loads = [
+        pltpu.make_async_copy(mask_hbm.at[:, pl.ds(base, loaded)], mask_window, sems.at[0]),
+        pltpu.make_async_copy(target_hbm.at[:, pl.ds(base, loaded)], target_window, sems.at[1]),
+    ]
+
+    def finish():
+        for load in loads:
+            load.wait()
+        clip_col = start + lax.broadcasted_iota(jnp.int32, (rows, width), 1)
+        col_inside = jnp.logical_and(clip_col >= 0, clip_col < clip_cols)
+        back = lax.rem(base - start + loaded, loaded)
+        mask_own = pltpu.roll(mask_window[...], back, 1)[:, :width]
+        mask_own = jnp.where(col_inside, mask_own, 0.0).astype(jnp.bfloat16)
+        target_own = pltpu.roll(target_window[...].astype(jnp.float32), back, 1)[:, :width]
+        return mask_own, target_own.astype(jnp.bfloat16)
+
+    return loads, finish
+
+
+def exchange_kernel(
+    sizes, mask_hbm, target_hbm, kernel_hbm, assign_hbm, all_taps, above, below,
+    mask_window, target_window, send_up, send_down, square, tap_rows, own_taps, kernel_ref,
+    assign_own, load_sem, own_sem, tap_send, tap_recv, halo_send, halo_recv,
 ):
-    kern_count, tile_count, span, share, width = sizes
+    kern_count, tile_count, span, share = sizes
     tile = lax.axis_index("tile")
     kern = lax.axis_index("kern")
-    rows, clip_cols = mask_hbm.shape
-    clip_rows = rows * tile_count
+    rows = mask_hbm.shape[0]
     margin = (span - 1) // 2
-    height = (rows + 2 * margin) // BLOCKS
-    padded = -(-height // 16) * 16
-    depth = toeplitz.shape[1]
-    reach = share + 4 * margin
-    lanes = shifted.shape[1]
+    depth = -(-span * PITCH // 128) * 128
     has_up = tile > 0
     has_down = tile < tile_count - 1
 
@@ -51,23 +72,14 @@
     def _():
         pl.semaphore_signal(barrier, inc=1, device_id=(tile + 1, kern), device_id_type=MESH)
 
-    start = kern * share - 2 * margin
-    loaded = width + 128
-    base = (start + 128) // 128 * 128 - 128
-    base = jnp.minimum(jnp.maximum(base, 0), clip_cols - loaded)
-    base = pl.multiple_of(base, 128)
     small_loads = [
         pltpu.make_async_copy(kernel_hbm, kernel_ref, load_sem.at[2]),
-        pltpu.make_async_copy(weight_hbm, weight_ref, load_sem.at[3]),
-        pltpu.make_async_copy(assign_hbm, assign_own, load_sem.at[4]),
+        pltpu.make_async_copy(assign_hbm, assign_own, load_sem.at[3]),
     ]
-    for load in small_loads:
-        load.start()
-    loads = [
-        pltpu.make_async_copy(mask_hbm.at[:, pl.ds(base, loaded)], mask_window, load_sem.at[0]),
-        pltpu.make_async_copy(target_hbm.at[:, pl.ds(base, loaded)], target_window, load_sem.at[1]),
-    ]
-    for load in loads:
+    loads, finish = window_of(
+        mask_hbm, target_hbm, mask_window, target_window, load_sem, share, margin
+    )
+    for load in small_loads + loads:
         load.start()
 
     square[...] = jnp.zeros_like(square)
@@ -97,15 +109,9 @@
             tap_rows[8 * part + chunk : 8 * part + chunk + 1, :] = chunks[chunk]
     own_taps[...] = tap_rows[...].astype(jnp.bfloat16)
 
-    for load in loads:
-        load.wait()
-    clip_col = start + lax.broadcasted_iota(jnp.int32, (rows, width), 1)
-    col_inside = jnp.logical_and(clip_col >= 0, clip_col < clip_cols)
-    back = lax.rem(base - start + loaded, loaded)
-    mask_own = pltpu.roll(mask_window[...], back, 1)[:, :width]
-    mask_own = jnp.where(col_inside, mask_own, 0.0).astype(jnp.bfloat16)
-    target_own = pltpu.roll(target_window[...].astype(jnp.float32), back, 1)[:, :width]
-    target_own = target_own.astype(jnp.bfloat16)
+    own_copy = pltpu.make_async_copy(own_taps, all_taps.at[0], own_sem)
+    own_copy.start()
+    mask_own, target_own = finish()
     send_up[0:MASK_HALO, :] = mask_own[0:MASK_HALO]
     send_up[MASK_HALO:, :] = target_own[0:TARGET_HALO]
     send_down[0:MASK_HALO, :] = mask_own[rows - MASK_HALO :]
@@ -144,29 +150,60 @@
         copy.start()
     pl.when(has_up)(upward.start)
     pl.when(has_down)(downward.start)
+    own_copy.wait()
+    for copy in tap_copies:
+        copy.wait()
+    pl.when(has_up)(upward.wait_send)
+    pl.when(has_down)(downward.wait_send)
+    pl.when(has_up)(downward.wait_recv)
+    pl.when(has_down)(upward.wait_recv)
+
+
+def gradient_kernel(
+    sizes, mask_hbm, target_hbm, weight_hbm, taps_hbm, above_hbm, below_hbm, grad_out, resist_out,
+    mask_window, target_window, weight_ref, all_taps, above, below, mask_rows, target_rows, toeplitz,
+    shifted, fields, adjoint, spread, resist_rows, grad_rows, resist_own, grad_own, load_sem, store_sem,
+):
+    kern_count, tile_count, span, share = sizes
+    tile = lax.axis_index("tile")
+    kern = lax.axis_index("kern")
+    rows, clip_cols = mask_hbm.shape
+    clip_rows = rows * tile_count
+    margin = (span - 1) // 2
+    height = (rows + 2 * margin) // BLOCKS
+    padded = -(-height // 16) * 16
+    depth = toeplitz.shape[1]
+    chunk_count = depth // 128
+    reach = share + 4 * margin
+    width = above.shape[1]
+    lanes = shifted.shape[1]
+
+    loads, finish = window_of(
+        mask_hbm, target_hbm, mask_window, target_window, load_sem, share, margin
+    )
+    halo_loads = [
+        pltpu.make_async_copy(above_hbm, above, load_sem.at[2]),
+        pltpu.make_async_copy(below_hbm, below, load_sem.at[3]),
+    ]
+    tap_loads = [
+        pltpu.make_async_copy(taps_hbm, all_taps, load_sem.at[4]),
+        pltpu.make_async_copy(weight_hbm, weight_ref, load_sem.at[5]),
+    ]
+    for load in loads + halo_loads + tap_loads:
+        load.start()
+
+    mask_own, target_own = finish()
     mask_rows[MASK_HALO : MASK_HALO + rows, :] = mask_own.astype(jnp.float32)
     target_rows[TARGET_HALO : TARGET_HALO + rows, :] = target_own.astype(jnp.float32)
-
-    @pl.when(has_up)
-    def _():
-        downward.wait_recv()
-
-    @pl.when(jnp.logical_not(has_up))
-    def _():
-        above[...] = jnp.zeros_like(above)
-
-    @pl.when(has_down)
-    def _():
-        upward.wait_recv()
-
-    @pl.when(jnp.logical_not(has_down))
-    def _():
-        below[...] = jnp.zeros_like(below)
-
-    mask_rows[0:MASK_HALO, :] = above[0:MASK_HALO, :].astype(jnp.float32)
-    mask_rows[MASK_HALO + rows :, :] = below[0:MASK_HALO, :].astype(jnp.float32)
-    target_rows[0:TARGET_HALO, :] = above[MASK_HALO:, :].astype(jnp.float32)
-    target_rows[TARGET_HALO + rows :, :] = below[MASK_HALO:, :].astype(jnp.float32)
+    for load in halo_loads:
+        load.wait()
+    for halo, inside, mask_at, target_at in (
+        (above, tile > 0, 0, 0),
+        (below, tile < tile_count - 1, MASK_HALO + rows, TARGET_HALO + rows),
+    ):
+        held = jnp.where(inside, halo[...].astype(jnp.float32), 0.0)
+        mask_rows[mask_at : mask_at + MASK_HALO, :] = held[0:MASK_HALO]
+        target_rows[target_at : target_at + TARGET_HALO, :] = held[MASK_HALO:]
 
     def side_by_side(held, top, count, shift):
         pieces = []
@@ -184,6 +221,8 @@
         shifted[column * PITCH : (column + 1) * PITCH, :] = turned.astype(jnp.bfloat16)
     shifted[span * PITCH :, :] = jnp.zeros((depth - span * PITCH, lanes), jnp.bfloat16)
 
+    for load in tap_loads:
+        load.wait()
     weights = weight_ref[...]
     total = jnp.sum(weights, axis=1, keepdims=True)
     slot_ids = lax.broadcasted_iota(jnp.int32, weights.shape, 1).astype(jnp.float32)
@@ -192,11 +231,7 @@
     same_chunk = own_lane >= own_row
     shares = []
     for source in range(kern_count):
-        if source == 0:
-            block = own_taps[...].astype(jnp.float32)
-        else:
-            tap_copies[source - 1].wait_recv()
-            block = all_taps[source].astype(jnp.float32)
+        block = all_taps[source].astype(jnp.float32)
         picked = jnp.where(slot_ids == block[7:8, 112:113], weights, 0.0)
         shares.append(jnp.sum(picked, axis=1, keepdims=True) / total)
         for part in range(2):
@@ -266,27 +301,8 @@
     grad_store = pltpu.make_async_copy(grad_own, grad_out, store_sem.at[1])
     grad_store.start()
 
-    for copy in tap_copies:
-        copy.wait_send()
-    pl.when(has_up)(upward.wait_send)
-    pl.when(has_down)(downward.wait_send)
     resist_store.wait()
     grad_store.wait()
-
-
-def hand_over_kernel(grad_in, resist_in, grad_out, resist_out, held, sems):
-    images = ((grad_in, grad_out), (resist_in, resist_out))
-    loads, stores = [], []
-    for at, (taken, given) in enumerate(images):
-        loads.append(pltpu.make_async_copy(taken, held.at[at], sems.at[at]))
-        stores.append(pltpu.make_async_copy(held.at[at], given, sems.at[2 + at]))
-    for load in loads:
-        load.start()
-    for load, store in zip(loads, stores):
-        load.wait()
-        store.start()
-    for store in stores:
-        store.wait()
 
 
 def on_device(mask, target, kernels, source_weight, assign):
@@ -304,23 +320,53 @@
     padded = -(-height // 16) * 16
     parts = 2 * kern_count
     halo = MASK_HALO + TARGET_HALO
-    image = jax.ShapeDtypeStruct((rows, share), jnp.float32)
-    images = pl.pallas_call(
-        functools.partial(gradient_kernel, (kern_count, tile_count, span, share, width)),
-        out_shape=(image, image),
-        in_specs=[IN_ANY] * 5,
-        out_specs=(IN_ANY, IN_ANY),
+    sizes = (kern_count, tile_count, span, share)
+    limit = 56 * 1024 * 1024
+    by_row = jnp.swapaxes(kernels[0], 0, 1)
+    taps, above, below = pl.pallas_call(
+        functools.partial(exchange_kernel, sizes),
+        out_shape=(
+            jax.ShapeDtypeStruct((kern_count, 16, 128), jnp.bfloat16),
+            jax.ShapeDtypeStruct((halo, width), jnp.bfloat16),
+            jax.ShapeDtypeStruct((halo, width), jnp.bfloat16),
+        ),
+        in_specs=[IN_ANY] * 4,
+        out_specs=(IN_ANY,) * 3,
         scratch_shapes=[
             pltpu.VMEM((rows, width + 128), jnp.float32),
             pltpu.VMEM((rows, width + 128), jnp.int32),
             pltpu.VMEM((halo, width), jnp.bfloat16),
             pltpu.VMEM((halo, width), jnp.bfloat16),
-            pltpu.VMEM((halo, width), jnp.bfloat16),
-            pltpu.VMEM((halo, width), jnp.bfloat16),
             pltpu.VMEM((2, 128, 128), jnp.float32),
             pltpu.VMEM((16, 128), jnp.float32),
             pltpu.VMEM((16, 128), jnp.bfloat16),
+            pltpu.VMEM(by_row.shape, by_row.dtype),
+            pltpu.SMEM((1,), jnp.int32),
+            pltpu.SemaphoreType.DMA((4,)),
+            pltpu.SemaphoreType.DMA,
+            pltpu.SemaphoreType.DMA((kern_count,)),
+            pltpu.SemaphoreType.DMA((kern_count,)),
+            pltpu.SemaphoreType.DMA((2,)),
+            pltpu.SemaphoreType.DMA((2,)),
+        ],
+        compiler_params=pltpu.CompilerParams(
+            collective_id=0, has_side_effects=True, vmem_limit_bytes=limit
+        ),
+        name="exchange",
+    )(mask, target, by_row, assign)
+    image = jax.ShapeDtypeStruct((rows, share), jnp.float32)
+    return pl.pallas_call(
+        functools.partial(gradient_kernel, sizes),
+        out_shape=(image, image),
+        in_specs=[IN_ANY] * 6,
+        out_specs=(IN_ANY, IN_ANY),
+        scratch_shapes=[
+            pltpu.VMEM((rows, width + 128), jnp.float32),
+            pltpu.VMEM((rows, width + 128), jnp.int32),
+            pltpu.VMEM((1, source_weight.shape[0]), jnp.float32),
             pltpu.VMEM((kern_count, 16, 128), jnp.bfloat16),
+            pltpu.VMEM((halo, width), jnp.bfloat16),
+            pltpu.VMEM((halo, width), jnp.bfloat16),
             pltpu.VMEM((rows + 2 * MASK_HALO, width), jnp.float32),
             pltpu.VMEM((rows + 2 * TARGET_HALO, width), jnp.float32),
             pltpu.VMEM((parts * padded, depth), jnp.bfloat16),
@@ -332,33 +378,12 @@
             pltpu.VMEM(((BLOCKS - 1) * height + PITCH, share), jnp.float32),
             pltpu.VMEM((rows, share), jnp.float32),
             pltpu.VMEM((rows, share), jnp.float32),
-            pltpu.VMEM(kernels.shape[2:3] + kernels.shape[1:2] + kernels.shape[3:], kernels.dtype),
-            pltpu.VMEM((1, source_weight.shape[0]), jnp.float32),
-            pltpu.SMEM((1,), jnp.int32),
-            pltpu.SemaphoreType.DMA((5,)),
-            pltpu.SemaphoreType.DMA((2,)),
-            pltpu.SemaphoreType.DMA((kern_count,)),
-            pltpu.SemaphoreType.DMA((kern_count,)),
-            pltpu.SemaphoreType.DMA((2,)),
+            pltpu.SemaphoreType.DMA((6,)),
             pltpu.SemaphoreType.DMA((2,)),
         ],
-        compiler_params=pltpu.CompilerParams(
-            collective_id=0, has_side_effects=True, vmem_limit_bytes=56 * 1024 * 1024
-        ),
+        compiler_params=pltpu.CompilerParams(vmem_limit_bytes=limit),
         name="image_gradient",
-    )(mask, target, jnp.swapaxes(kernels[0], 0, 1), source_weight[None, :], assign)
-    return pl.pallas_call(
-        hand_over_kernel,
-        out_shape=(image, image),
-        in_specs=[IN_ANY, IN_ANY],
-        out_specs=(IN_ANY, IN_ANY),
-        scratch_shapes=[
-            pltpu.VMEM((2, rows, share), jnp.float32),
-            pltpu.SemaphoreType.DMA((4,)),
-        ],
-        compiler_params=pltpu.CompilerParams(vmem_limit_bytes=56 * 1024 * 1024),
-        name="hand_over",
-    )(*images)
+    )(mask, target, source_weight[None, :], taps, above, below)
 
 
 def solution(mesh):

time: 17.1 us -> 16 us (0.936)
  Pallas kernels: 15.6 us -> 14.5 us
    pallas_call x2, Pallas kernels: 15.6 us -> 14.5 us  [the longest x1 9.16 us: on_device(): pl.pallas_call(functools.partial(exchange_kernel, sizes), out_shape=(jax....]
where the time goes in v6:
time: 16 us; the launch traced here: 15.8 us
  Pallas kernels  14.5 us (91%)
  between operations  1.28 us (8%)
    pallas_call x1, Pallas kernels, on_device(): pl.pallas_call(functools.partial(exchange_kernel, sizes), out_shape=(jax....  9.16 us
    pallas_call x1, Pallas kernels, on_device(): pl.pallas_call(functools.partial(gradient_kernel, sizes), out_shape=(imag...  5.31 us

profile of v6, /device:TPU:1, one launch (start us, length us, event | category | flops | bytes accessed | tf_op | source)
XLA Modules:
  0.0 15.8 jit_solution(16298096526253321213)
XLA Ops:
  1.3 9.2 %exchange.1 = (bf16[8,16,128]{2,1,0:T(8,128)(2,1)}, bf16[48,384]{1,0:T(8,128)(2,1)}, bf16[48,384]{1,0:T(8,128)(2,1)}) custom-call(f32[64,2048]{1,0:T(8,128)} %mask_hbm.3, s32[64,2048]{1,0:T(8,128)} %target_hbm.3, bf16[21,2,21]{2,1,0:T(2,128)(2,1)} %bitcast.4, s32[1]{0:T(128)S(6)} %copy.7.assign_hbm), custom_call_target="tpu_custom_call" | custom-call | tf_op jit(solution)/shard_map/exchange/pallas_call | solution.py:326
  10.4 5.3 %image_gradient.1 = (f32[64,256]{1,0:T(8,128)}, f32[64,256]{1,0:T(8,128)}) custom-call(f32[64,2048]{1,0:T(8,128)} %mask_hbm.3, s32[64,2048]{1,0:T(8,128)} %target_hbm.3, f32[1,8]{1,0:T(1,128)} %bitcast.5, bf16[8,16,128]{2,1,0:T(8,128)(2,1)} %get-tuple-element.5.taps_hbm, bf16[48,384]{1,0:T(8,128)(2,1)} %get-tuple-element.6.above_hbm, ...), custom_call_target="tpu_custom_call" | custom-call | tf_op jit(solution)/shard_map/image_gradient/pallas_call | solution.py:358

commit v7 on v6

--- a/solution.py
+++ b/solution.py
@@ -111,11 +111,6 @@
 
     own_copy = pltpu.make_async_copy(own_taps, all_taps.at[0], own_sem)
     own_copy.start()
-    mask_own, target_own = finish()
-    send_up[0:MASK_HALO, :] = mask_own[0:MASK_HALO]
-    send_up[MASK_HALO:, :] = target_own[0:TARGET_HALO]
-    send_down[0:MASK_HALO, :] = mask_own[rows - MASK_HALO :]
-    send_down[MASK_HALO:, :] = target_own[rows - TARGET_HALO :]
     upward = pltpu.make_async_remote_copy(
         src_ref=send_up,
         dst_ref=below,
@@ -148,6 +143,11 @@
         )
     for copy in tap_copies:
         copy.start()
+    mask_own, target_own = finish()
+    send_up[0:MASK_HALO, :] = mask_own[0:MASK_HALO]
+    send_up[MASK_HALO:, :] = target_own[0:TARGET_HALO]
+    send_down[0:MASK_HALO, :] = mask_own[rows - MASK_HALO :]
+    send_down[MASK_HALO:, :] = target_own[rows - TARGET_HALO :]
     pl.when(has_up)(upward.start)
     pl.when(has_down)(downward.start)
     own_copy.wait()
@@ -162,7 +162,8 @@
 def gradient_kernel(
     sizes, mask_hbm, target_hbm, weight_hbm, taps_hbm, above_hbm, below_hbm, grad_out, resist_out,
     mask_window, target_window, weight_ref, all_taps, above, below, mask_rows, target_rows, toeplitz,
-    shifted, fields, adjoint, spread, resist_rows, grad_rows, resist_own, grad_own, load_sem, store_sem,
+    shifted, fields, adjoint, spread, resist_rows, grad_rows, resist_own, grad_own, flipped, resist_wide,
+    load_sem, store_sem,
 ):
     kern_count, tile_count, span, share = sizes
     tile = lax.axis_index("tile")
@@ -246,48 +247,54 @@
                 ).astype(jnp.bfloat16)
                 before = turned
 
-    fields[...] = jnp.dot(toeplitz[...], shifted[...], preferred_element_type=jnp.float32)
-
-    row_at = lax.broadcasted_iota(jnp.int32, (padded, lanes), 0)
-    col_at = lax.broadcasted_iota(jnp.int32, (padded, lanes), 1)
-    clip_row = tile * rows - margin + row_at
-    clip_col = kern * share - margin + col_at
-    for block in range(1, BLOCKS):
-        later = col_at >= block * reach
-        clip_row = jnp.where(later, clip_row + height, clip_row)
-        clip_col = jnp.where(later, clip_col - reach, clip_col)
-    inside = jnp.logical_and(
-        jnp.logical_and(clip_row >= 0, clip_row < clip_rows),
-        jnp.logical_and(clip_col >= 0, clip_col < clip_cols),
-    )
-    inside = jnp.logical_and(inside, row_at < height)
+    flipped[...] = toeplitz[...].T
     target = side_by_side(target_rows, TARGET_HALO - margin, padded, margin)
-    aerial = jnp.zeros((padded, lanes), jnp.float32)
-    for source in range(kern_count):
-        first = 2 * source * padded
-        real = fields[first : first + padded, :]
-        imag = fields[first + padded : first + 2 * padded, :]
-        aerial = aerial + shares[source] * (real * real + imag * imag)
-    resist = 1.0 / (1.0 + jnp.exp(-SLOPE_FACTOR * (aerial - LEVEL_VALUE)))
-    sense = 2.0 * (resist - target) * SLOPE_FACTOR * resist * (1.0 - resist)
-    sense = jnp.where(inside, sense, 0.0)
-    for source in range(kern_count):
-        scaled = (2.0 * shares[source]) * sense
-        for part in range(2):
-            first = (2 * source + part) * padded
-            adjoint[first : first + padded, :] = (
-                scaled * fields[first : first + padded, :]
-            ).astype(jnp.bfloat16)
+    for tile_at in range(0, lanes, 256):
+        tile_lanes = slice(tile_at, min(tile_at + 256, lanes))
+        count = min(256, lanes - tile_at)
+        fields[:, tile_lanes] = jnp.dot(
+            toeplitz[...], shifted[:, tile_lanes], preferred_element_type=jnp.float32
+        )
+        row_at = lax.broadcasted_iota(jnp.int32, (padded, count), 0)
+        col_at = lax.broadcasted_iota(jnp.int32, (padded, count), 1) + tile_at
+        clip_row = tile * rows - margin + row_at
+        clip_col = kern * share - margin + col_at
+        for block in range(1, BLOCKS):
+            later = col_at >= block * reach
+            clip_row = jnp.where(later, clip_row + height, clip_row)
+            clip_col = jnp.where(later, clip_col - reach, clip_col)
+        inside = jnp.logical_and(
+            jnp.logical_and(clip_row >= 0, clip_row < clip_rows),
+            jnp.logical_and(clip_col >= 0, clip_col < clip_cols),
+        )
+        inside = jnp.logical_and(inside, row_at < height)
+        aerial = jnp.zeros((padded, count), jnp.float32)
+        for source in range(kern_count):
+            first = 2 * source * padded
+            real = fields[first : first + padded, tile_lanes]
+            imag = fields[first + padded : first + 2 * padded, tile_lanes]
+            aerial = aerial + shares[source] * (real * real + imag * imag)
+        resist = 1.0 / (1.0 + jnp.exp(-SLOPE_FACTOR * (aerial - LEVEL_VALUE)))
+        resist_wide[:, tile_lanes] = resist
+        sense = 2.0 * (resist - target[:, tile_lanes]) * SLOPE_FACTOR * resist * (1.0 - resist)
+        sense = jnp.where(inside, sense, 0.0)
+        for source in range(kern_count):
+            scaled = (2.0 * shares[source]) * sense
+            for part in range(2):
+                first = (2 * source + part) * padded
+                adjoint[first : first + padded, tile_lanes] = (
+                    scaled * fields[first : first + padded, tile_lanes]
+                ).astype(jnp.bfloat16)
+        spread[:, tile_lanes] = jnp.dot(
+            flipped[...], adjoint[:, tile_lanes], preferred_element_type=jnp.float32
+        )
+    resist = resist_wide[...]
     for block in range(BLOCKS):
         piece = pltpu.roll(resist, lanes - block * reach - margin, 1)[:, :share]
         resist_rows[block * height : block * height + padded, :] = piece
     resist_own[...] = resist_rows[margin : margin + rows, :]
     resist_store = pltpu.make_async_copy(resist_own, resist_out, store_sem.at[0])
     resist_store.start()
-
-    spread[...] = lax.dot_general(
-        toeplitz[...], adjoint[...], (((0,), (0,)), ((), ())), preferred_element_type=jnp.float32
-    )
 
     gathered = spread[0:PITCH, :]
     for column in range(1, span):
@@ -378,6 +385,8 @@
             pltpu.VMEM(((BLOCKS - 1) * height + PITCH, share), jnp.float32),
             pltpu.VMEM((rows, share), jnp.float32),
             pltpu.VMEM((rows, share), jnp.float32),
+            pltpu.VMEM((depth, parts * padded), jnp.bfloat16),
+            pltpu.VMEM((padded, lanes), jnp.float32),
             pltpu.SemaphoreType.DMA((6,)),
             pltpu.SemaphoreType.DMA((2,)),
         ],

time: 16 us -> 16.7 us (1.044)
  Pallas kernels: 14.5 us -> 15.2 us
    pallas_call x1, Pallas kernels: 5.31 us -> 5.87 us  [on_device(): pl.pallas_call(functools.partial(gradient_kernel, sizes), out_shape=(imag...]
where the time goes in v7:
time: 16.7 us; the launch traced here: 16.4 us
  Pallas kernels  15.2 us (91%)
  between operations  1.28 us (8%)
    pallas_call x1, Pallas kernels, on_device(): pl.pallas_call(functools.partial(exchange_kernel, sizes), out_shape=(jax....  9.28 us
    pallas_call x1, Pallas kernels, on_device(): pl.pallas_call(functools.partial(gradient_kernel, sizes), out_shape=(imag...  5.87 us

profile of v7, /device:TPU:1, one launch (start us, length us, event | category | flops | bytes accessed | tf_op | source)
XLA Modules:
  0.0 16.4 jit_solution(5205295014187020420)
XLA Ops:
  1.3 9.3 %exchange.1 = (bf16[8,16,128]{2,1,0:T(8,128)(2,1)}, bf16[48,384]{1,0:T(8,128)(2,1)}, bf16[48,384]{1,0:T(8,128)(2,1)}) custom-call(f32[64,2048]{1,0:T(8,128)} %mask_hbm.3, s32[64,2048]{1,0:T(8,128)} %target_hbm.3, bf16[21,2,21]{2,1,0:T(2,128)(2,1)} %bitcast.4, s32[1]{0:T(128)S(6)} %copy.7.assign_hbm), custom_call_target="tpu_custom_call" | custom-call | tf_op jit(solution)/shard_map/exchange/pallas_call | solution.py:333
  10.6 5.9 %image_gradient.1 = (f32[64,256]{1,0:T(8,128)}, f32[64,256]{1,0:T(8,128)}) custom-call(f32[64,2048]{1,0:T(8,128)} %mask_hbm.3, s32[64,2048]{1,0:T(8,128)} %target_hbm.3, f32[1,8]{1,0:T(1,128)} %bitcast.5, bf16[8,16,128]{2,1,0:T(8,128)(2,1)} %get-tuple-element.5.taps_hbm, bf16[48,384]{1,0:T(8,128)(2,1)} %get-tuple-element.6.above_hbm, ...), custom_call_target="tpu_custom_call" | custom-call | tf_op jit(solution)/shard_map/image_gradient/pallas_call | solution.py:365

commit v8 on v6

--- a/solution.py
+++ b/solution.py
@@ -111,11 +111,6 @@
 
     own_copy = pltpu.make_async_copy(own_taps, all_taps.at[0], own_sem)
     own_copy.start()
-    mask_own, target_own = finish()
-    send_up[0:MASK_HALO, :] = mask_own[0:MASK_HALO]
-    send_up[MASK_HALO:, :] = target_own[0:TARGET_HALO]
-    send_down[0:MASK_HALO, :] = mask_own[rows - MASK_HALO :]
-    send_down[MASK_HALO:, :] = target_own[rows - TARGET_HALO :]
     upward = pltpu.make_async_remote_copy(
         src_ref=send_up,
         dst_ref=below,
@@ -148,6 +143,11 @@
         )
     for copy in tap_copies:
         copy.start()
+    mask_own, target_own = finish()
+    send_up[0:MASK_HALO, :] = mask_own[0:MASK_HALO]
+    send_up[MASK_HALO:, :] = target_own[0:TARGET_HALO]
+    send_down[0:MASK_HALO, :] = mask_own[rows - MASK_HALO :]
+    send_down[MASK_HALO:, :] = target_own[rows - TARGET_HALO :]
     pl.when(has_up)(upward.start)
     pl.when(has_down)(downward.start)
     own_copy.wait()
@@ -162,7 +162,8 @@
 def gradient_kernel(
     sizes, mask_hbm, target_hbm, weight_hbm, taps_hbm, above_hbm, below_hbm, grad_out, resist_out,
     mask_window, target_window, weight_ref, all_taps, above, below, mask_rows, target_rows, toeplitz,
-    shifted, fields, adjoint, spread, resist_rows, grad_rows, resist_own, grad_own, load_sem, store_sem,
+    shifted, fields, adjoint, spread, resist_rows, grad_rows, resist_own, grad_own, flipped,
+    load_sem, store_sem,
 ):
     kern_count, tile_count, span, share = sizes
     tile = lax.axis_index("tile")
@@ -246,6 +247,7 @@
                 ).astype(jnp.bfloat16)
                 before = turned
 
+    flipped[...] = toeplitz[...].T
     fields[...] = jnp.dot(toeplitz[...], shifted[...], preferred_element_type=jnp.float32)
 
     row_at = lax.broadcasted_iota(jnp.int32, (padded, lanes), 0)
@@ -285,9 +287,7 @@
     resist_store = pltpu.make_async_copy(resist_own, resist_out, store_sem.at[0])
     resist_store.start()
 
-    spread[...] = lax.dot_general(
-        toeplitz[...], adjoint[...], (((0,), (0,)), ((), ())), preferred_element_type=jnp.float32
-    )
+    spread[...] = jnp.dot(flipped[...], adjoint[...], preferred_element_type=jnp.float32)
 
     gathered = spread[0:PITCH, :]
     for column in range(1, span):
@@ -378,6 +378,7 @@
             pltpu.VMEM(((BLOCKS - 1) * height + PITCH, share), jnp.float32),
             pltpu.VMEM((rows, share), jnp.float32),
             pltpu.VMEM((rows, share), jnp.float32),
+            pltpu.VMEM((depth, parts * padded), jnp.bfloat16),
             pltpu.SemaphoreType.DMA((6,)),
             pltpu.SemaphoreType.DMA((2,)),
         ],

time: 16 us -> 16.1 us (level)
  no operation moved by 1% of the time
where the time goes in v8:
time: 16.1 us; the launch traced here: 15.9 us
  Pallas kernels  14.6 us (91%)
  between operations  1.28 us (8%)
    pallas_call x1, Pallas kernels, on_device(): pl.pallas_call(functools.partial(exchange_kernel, sizes), out_shape=(jax....  9.28 us
    pallas_call x1, Pallas kernels, on_device(): pl.pallas_call(functools.partial(gradient_kernel, sizes), out_shape=(imag...  5.29 us

profile of v8, /device:TPU:1, one launch (start us, length us, event | category | flops | bytes accessed | tf_op | source)
XLA Modules:
  0.0 15.9 jit_solution(3351440114935764203)
XLA Ops:
  1.3 9.3 %exchange.1 = (bf16[8,16,128]{2,1,0:T(8,128)(2,1)}, bf16[48,384]{1,0:T(8,128)(2,1)}, bf16[48,384]{1,0:T(8,128)(2,1)}) custom-call(f32[64,2048]{1,0:T(8,128)} %mask_hbm.3, s32[64,2048]{1,0:T(8,128)} %target_hbm.3, bf16[21,2,21]{2,1,0:T(2,128)(2,1)} %bitcast.4, s32[1]{0:T(128)S(6)} %copy.7.assign_hbm), custom_call_target="tpu_custom_call" | custom-call | tf_op jit(solution)/shard_map/exchange/pallas_call | solution.py:326
  10.6 5.3 %image_gradient.1 = (f32[64,256]{1,0:T(8,128)}, f32[64,256]{1,0:T(8,128)}) custom-call(f32[64,2048]{1,0:T(8,128)} %mask_hbm.3, s32[64,2048]{1,0:T(8,128)} %target_hbm.3, f32[1,8]{1,0:T(1,128)} %bitcast.5, bf16[8,16,128]{2,1,0:T(8,128)(2,1)} %get-tuple-element.5.taps_hbm, bf16[48,384]{1,0:T(8,128)(2,1)} %get-tuple-element.6.above_hbm, ...), custom_call_target="tpu_custom_call" | custom-call | tf_op jit(solution)/shard_map/image_gradient/pallas_call | solution.py:358

commit v9 on v6

--- a/solution.py
+++ b/solution.py
@@ -46,9 +46,9 @@
 
 
 def exchange_kernel(
-    sizes, mask_hbm, target_hbm, kernel_hbm, assign_hbm, all_taps, above, below,
+    sizes, mask_hbm, target_hbm, kernel_hbm, assign_hbm, all_taps, above, below, own_rows,
     mask_window, target_window, send_up, send_down, square, tap_rows, own_taps, kernel_ref,
-    assign_own, load_sem, own_sem, tap_send, tap_recv, halo_send, halo_recv,
+    assign_own, own_image, load_sem, own_sem, tap_send, tap_recv, halo_send, halo_recv,
 ):
     kern_count, tile_count, span, share = sizes
     tile = lax.axis_index("tile")
@@ -109,9 +109,13 @@
             tap_rows[8 * part + chunk : 8 * part + chunk + 1, :] = chunks[chunk]
     own_taps[...] = tap_rows[...].astype(jnp.bfloat16)
 
-    own_copy = pltpu.make_async_copy(own_taps, all_taps.at[0], own_sem)
+    own_copy = pltpu.make_async_copy(own_taps, all_taps.at[0], own_sem.at[0])
     own_copy.start()
     mask_own, target_own = finish()
+    own_image[0:rows, :] = mask_own
+    own_image[rows:, :] = target_own
+    image_copy = pltpu.make_async_copy(own_image, own_rows, own_sem.at[1])
+    image_copy.start()
     send_up[0:MASK_HALO, :] = mask_own[0:MASK_HALO]
     send_up[MASK_HALO:, :] = target_own[0:TARGET_HALO]
     send_down[0:MASK_HALO, :] = mask_own[rows - MASK_HALO :]
@@ -151,6 +155,7 @@
     pl.when(has_up)(upward.start)
     pl.when(has_down)(downward.start)
     own_copy.wait()
+    image_copy.wait()
     for copy in tap_copies:
         copy.wait()
     pl.when(has_up)(upward.wait_send)
@@ -160,14 +165,14 @@
 
 
 def gradient_kernel(
-    sizes, mask_hbm, target_hbm, weight_hbm, taps_hbm, above_hbm, below_hbm, grad_out, resist_out,
-    mask_window, target_window, weight_ref, all_taps, above, below, mask_rows, target_rows, toeplitz,
+    sizes, own_hbm, weight_hbm, taps_hbm, above_hbm, below_hbm, grad_out, resist_out,
+    own_image, weight_ref, all_taps, above, below, mask_rows, target_rows, toeplitz,
     shifted, fields, adjoint, spread, resist_rows, grad_rows, resist_own, grad_own, load_sem, store_sem,
 ):
-    kern_count, tile_count, span, share = sizes
+    kern_count, tile_count, span, share, clip_cols = sizes
     tile = lax.axis_index("tile")
     kern = lax.axis_index("kern")
-    rows, clip_cols = mask_hbm.shape
+    rows = own_hbm.shape[0] // 2
     clip_rows = rows * tile_count
     margin = (span - 1) // 2
     height = (rows + 2 * margin) // BLOCKS
@@ -178,9 +183,7 @@
     width = above.shape[1]
     lanes = shifted.shape[1]
 
-    loads, finish = window_of(
-        mask_hbm, target_hbm, mask_window, target_window, load_sem, share, margin
-    )
+    own_load = pltpu.make_async_copy(own_hbm, own_image, load_sem.at[0])
     halo_loads = [
         pltpu.make_async_copy(above_hbm, above, load_sem.at[2]),
         pltpu.make_async_copy(below_hbm, below, load_sem.at[3]),
@@ -189,12 +192,12 @@
         pltpu.make_async_copy(taps_hbm, all_taps, load_sem.at[4]),
         pltpu.make_async_copy(weight_hbm, weight_ref, load_sem.at[5]),
     ]
-    for load in loads + halo_loads + tap_loads:
+    for load in [own_load] + halo_loads + tap_loads:
         load.start()
 
-    mask_own, target_own = finish()
-    mask_rows[MASK_HALO : MASK_HALO + rows, :] = mask_own.astype(jnp.float32)
-    target_rows[TARGET_HALO : TARGET_HALO + rows, :] = target_own.astype(jnp.float32)
+    own_load.wait()
+    mask_rows[MASK_HALO : MASK_HALO + rows, :] = own_image[0:rows, :].astype(jnp.float32)
+    target_rows[TARGET_HALO : TARGET_HALO + rows, :] = own_image[rows:, :].astype(jnp.float32)
     for load in halo_loads:
         load.wait()
     for halo, inside, mask_at, target_at in (
@@ -323,15 +326,16 @@
     sizes = (kern_count, tile_count, span, share)
     limit = 56 * 1024 * 1024
     by_row = jnp.swapaxes(kernels[0], 0, 1)
-    taps, above, below = pl.pallas_call(
+    taps, above, below, own_rows = pl.pallas_call(
         functools.partial(exchange_kernel, sizes),
         out_shape=(
             jax.ShapeDtypeStruct((kern_count, 16, 128), jnp.bfloat16),
             jax.ShapeDtypeStruct((halo, width), jnp.bfloat16),
             jax.ShapeDtypeStruct((halo, width), jnp.bfloat16),
+            jax.ShapeDtypeStruct((2 * rows, width), jnp.bfloat16),
         ),
         in_specs=[IN_ANY] * 4,
-        out_specs=(IN_ANY,) * 3,
+        out_specs=(IN_ANY,) * 4,
         scratch_shapes=[
             pltpu.VMEM((rows, width + 128), jnp.float32),
             pltpu.VMEM((rows, width + 128), jnp.int32),
@@ -342,8 +346,9 @@
             pltpu.VMEM((16, 128), jnp.bfloat16),
             pltpu.VMEM(by_row.shape, by_row.dtype),
             pltpu.SMEM((1,), jnp.int32),
+            pltpu.VMEM((2 * rows, width), jnp.bfloat16),
             pltpu.SemaphoreType.DMA((4,)),
-            pltpu.SemaphoreType.DMA,
+            pltpu.SemaphoreType.DMA((2,)),
             pltpu.SemaphoreType.DMA((kern_count,)),
             pltpu.SemaphoreType.DMA((kern_count,)),
             pltpu.SemaphoreType.DMA((2,)),
@@ -356,13 +361,12 @@
     )(mask, target, by_row, assign)
     image = jax.ShapeDtypeStruct((rows, share), jnp.float32)
     return pl.pallas_call(
-        functools.partial(gradient_kernel, sizes),
+        functools.partial(gradient_kernel, sizes + (col_count,)),
         out_shape=(image, image),
-        in_specs=[IN_ANY] * 6,
+        in_specs=[IN_ANY] * 5,
         out_specs=(IN_ANY, IN_ANY),
         scratch_shapes=[
-            pltpu.VMEM((rows, width + 128), jnp.float32),
-            pltpu.VMEM((rows, width + 128), jnp.int32),
+            pltpu.VMEM((2 * rows, width), jnp.bfloat16),
             pltpu.VMEM((1, source_weight.shape[0]), jnp.float32),
             pltpu.VMEM((kern_count, 16, 128), jnp.bfloat16),
             pltpu.VMEM((halo, width), jnp.bfloat16),
@@ -383,7 +387,7 @@
         ],
         compiler_params=pltpu.CompilerParams(vmem_limit_bytes=limit),
         name="image_gradient",
-    )(mask, target, source_weight[None, :], taps, above, below)
+    )(own_rows, source_weight[None, :], taps, above, below)
 
 
 def solution(mesh):

time: 16 us -> 15.8 us (0.988)
  Pallas kernels: 14.5 us -> 14.3 us
    pallas_call x1, Pallas kernels: 5.31 us -> 5.08 us  [on_device(): pl.pallas_call(functools.partial(gradient_kernel, sizes + (col_count,)),...]
where the time goes in v9:
time: 15.8 us; the launch traced here: 15.5 us
  Pallas kernels  14.3 us (91%)
  between operations  1.28 us (8%)
    pallas_call x1, Pallas kernels, on_device(): pl.pallas_call(functools.partial(exchange_kernel, sizes), out_shape=(jax....  9.17 us
    pallas_call x1, Pallas kernels, on_device(): pl.pallas_call(functools.partial(gradient_kernel, sizes + (col_count,)),...  5.08 us

profile of v9, /device:TPU:1, one launch (start us, length us, event | category | flops | bytes accessed | tf_op | source)
XLA Modules:
  0.0 15.5 jit_solution(1257192557353674535)
XLA Ops:
  1.3 9.2 %exchange.1 = (bf16[8,16,128]{2,1,0:T(8,128)(2,1)}, bf16[48,384]{1,0:T(8,128)(2,1)}, bf16[48,384]{1,0:T(8,128)(2,1)}, bf16[128,384]{1,0:T(8,128)(2,1)}) custom-call(f32[64,2048]{1,0:T(8,128)} %mask_hbm.1, s32[64,2048]{1,0:T(8,128)} %target_hbm.1, bf16[21,2,21]{2,1,0:T(2,128)(2,1)} %bitcast.4, s32[1]{0:T(128)S(6)} %copy.7.assign_hbm), custom_call_target="tpu_custom_call" | custom-call | tf_op jit(solution)/shard_map/exchange/pallas_call | solution.py:329
  10.5 5.1 %image_gradient.1 = (f32[64,256]{1,0:T(8,128)}, f32[64,256]{1,0:T(8,128)}) custom-call(bf16[128,384]{1,0:T(8,128)(2,1)} %get-tuple-element.6.own_hbm, f32[1,8]{1,0:T(1,128)} %bitcast.5, bf16[8,16,128]{2,1,0:T(8,128)(2,1)} %get-tuple-element.7.taps_hbm, bf16[48,384]{1,0:T(8,128)(2,1)} %get-tuple-element.8.above_hbm, bf16[48,384]{1,0:T(8,128)(2,1)} %get-tuple-element.9.below_hbm), custom_call_target="tpu_custom_call" | custom-call | tf_op jit(solution)/shard_map/image_gradient/pallas_call | solution.py:363
